TPU v7x, 128 devices: a whole 4x4x4 slice. The times are simulated.
128 devices in a mesh: lat: 8 (over x, core), lon: 16 (over z, y).
Axes of the slice: x: 4, y: 4, z: 4, core: 2. Of those that a mesh axis runs over, the one named last changes fastest.
Arguments:
- fields: bfloat16 [720, 1440, 256], P('lat', 'lon'), may hold values from -6 to 6
- spectral_gain: float32 [720, 2, 256], replicated, may hold values from -6 to 6
- mix_weight: bfloat16 [2, 256, 256], replicated, may hold values from -0.25 to 0.25
- column_list: int32 [720], replicated, may hold values from 0 to 719, each once
- column_counts: int32 [128], replicated, may hold values from 1 to 7, 720 in all
Outputs:
- blended: bfloat16 [720, 1440, 256], P('lat', 'lon')
- spectrum: bfloat16 [128, 7, 720, 2, 256], P(('lat', 'lon'))
Inputs may be any that keep to these rules, and one draw needn't show every extreme that they name: `column_list`: a permutation of the 720 orders. `column_counts`: the counts sum to 720; the largest is exactly 7.
All inputs are finite; a program needn't handle non-finite values.
Results may differ from a plain program's by a relative error of at most 0.012.
Values may be sent and summed in bfloat16 or wider, within the bound.
No kernel may reach another device: no remote copies, remote signals or barrier semaphores. Data moves between devices by JAX's collectives and lax.ppermute only.
A program may use at most 192 MiB of HBM per device.

v0:
```python
import math

import jax
import jax.numpy as jnp
from jax import lax
from jax.sharding import PartitionSpec as P


def latitudes(total_rows, first_row, band_rows):
    position = (first_row + jnp.arange(band_rows, dtype=jnp.int32)).astype(jnp.float32)
    colatitude = math.pi * (position + 0.5) / total_rows
    return (jnp.cos(colatitude), jnp.sin(colatitude), math.pi / total_rows * jnp.sin(colatitude))


def fourier_table(orders, live_mask, lon_total):
    longitude = jnp.arange(lon_total, dtype=jnp.int32)
    wrapped = longitude[:, None] * orders[None, :] % lon_total
    angles = wrapped.astype(jnp.float32) * (2.0 * math.pi / lon_total)
    stacked = jnp.stack([jnp.cos(angles), -jnp.sin(angles)], axis=2)
    return (stacked * live_mask[None, :, None]).astype(jnp.bfloat16)


def legendre_blocks(orders, cosines, sines, degrees):
    order_col = orders[:, None]
    half_gamma = 0.5 * math.log(math.pi) - math.log(2.0)
    log_start = (
        -0.5 * math.log(2.0)
        + 0.5 * (lax.lgamma(order_col + 1.5) - half_gamma - lax.lgamma(order_col + 1.0))
        + order_col * jnp.log(sines)[None, :]
    )
    zeros_now = jnp.zeros(log_start.shape, jnp.float32)
    ones_now = jnp.ones(log_start.shape, jnp.float32)
    block = math.gcd(degrees, 16)
    buffer = jnp.zeros((log_start.shape[0], degrees, log_start.shape[1]), jnp.bfloat16)

    def advance(previous, current, log_scale, level):
        upper = jnp.sqrt(
            jnp.maximum(4.0 * level * level - 1.0, 0.0)
            / jnp.maximum(level * level - order_col * order_col, 1.0)
        )
        lower = jnp.sqrt(
            jnp.maximum((level - 1.0) ** 2 - order_col * order_col, 0.0)
            / jnp.maximum(4.0 * (level - 1.0) ** 2 - 1.0, 1.0)
        )
        advanced = upper * (cosines[None, :] * current - lower * previous)
        largest = jnp.maximum(jnp.abs(advanced), jnp.abs(current))
        moving = level > order_col
        safe_largest = jnp.where(moving, largest, 1.0)
        previous_new = jnp.where(moving, current / safe_largest, previous)
        current_new = jnp.where(moving, advanced / safe_largest, current)
        scale_new = jnp.where(moving, log_scale + jnp.log(safe_largest), log_scale)
        values_now = jnp.where(level < order_col, 0.0, current_new * jnp.exp(scale_new))
        return (previous_new, current_new, scale_new, values_now)

    def fill_block(index, state):
        previous, current, log_scale, table = state
        first = index * block
        rows_now = []
        for inner in range(block):
            level = (first + inner).astype(jnp.float32)
            previous, current, log_scale, values_now = advance(previous, current, log_scale, level)
            rows_now.append(values_now)
        tile = jnp.stack(rows_now, axis=1).astype(jnp.bfloat16)
        table = lax.dynamic_update_slice(
            table, tile, (jnp.int32(0), first.astype(jnp.int32), jnp.int32(0))
        )
        return (previous, current, log_scale, table)

    initial = (zeros_now, ones_now, log_start, buffer)
    _, _, _, table = lax.fori_loop(0, degrees // block, fill_block, initial)
    return table


def apply_gain(spectra, spectral_gain):
    channels = spectral_gain.shape[2]
    real_part = spectra[..., :channels]
    imag_part = spectra[..., channels:]
    gain_real = spectral_gain[:, 0, :]
    gain_imag = spectral_gain[:, 1, :]
    return jnp.concatenate(
        [
            gain_real * real_part - gain_imag * imag_part,
            gain_real * imag_part + gain_imag * real_part,
        ],
        axis=-1,
    )


def complex_block(mix_weight):
    top_half = jnp.concatenate([mix_weight[0], mix_weight[1]], axis=1)
    bottom_half = jnp.concatenate([-mix_weight[1], mix_weight[0]], axis=1)
    return jnp.concatenate([top_half, bottom_half], axis=0)


def shards(fields, spectral_gain, mix_weight, column_list, column_counts):
    lat_rows, lon_cols, channels = fields.shape
    lat_devices = lax.axis_size("lat")
    lon_devices = lax.axis_size("lon")
    owners = lat_devices * lon_devices
    lat_total = lat_rows * lat_devices
    lon_total = lon_cols * lon_devices
    group_width = channels // lon_devices
    degrees = spectral_gain.shape[0]
    mode_count = column_list.shape[0]
    slot_count = (mode_count + owners - 1) // owners + 1
    run_ends = jnp.cumsum(column_counts)
    starts = run_ends - column_counts
    offsets = jnp.arange(slot_count, dtype=jnp.int32)
    positions = jnp.minimum(starts[:, None] + offsets[None, :], mode_count - 1).reshape(-1)
    live_mask = (offsets[None, :] < column_counts[:, None]).astype(jnp.float32).reshape(-1)
    matches = positions[:, None] == jnp.arange(mode_count, dtype=jnp.int32)[None, :]
    slot_orders = jnp.sum(jnp.where(matches, column_list[None, :], 0), axis=1)
    fourier = fourier_table(slot_orders, live_mask, lon_total)
    owner_index = lax.axis_index(("lat", "lon"))
    own_orders = lax.dynamic_slice_in_dim(slot_orders, owner_index * slot_count, slot_count)
    cosines, sines, _ = latitudes(lat_total, 0, lat_total)
    associated = legendre_blocks(own_orders.astype(jnp.float32), cosines, sines, degrees)
    channel_first = fields.transpose(2, 0, 1)
    summed = jnp.einsum(
        "caj,jsp->spca",
        lax.all_to_all(channel_first, "lon", split_axis=0, concat_axis=2, tiled=True),
        fourier,
        preferred_element_type=jnp.float32,
    )
    _, _, row_weights = latitudes(lat_total, lax.axis_index("lat") * lat_rows, lat_rows)
    spectral_in = (summed * row_weights[None, None, None, :]).astype(jnp.bfloat16)
    outgoing = spectral_in.reshape(owners, slot_count, 2, group_width, lat_rows)
    arrived = lax.all_to_all(outgoing, ("lat", "lon"), split_axis=0, concat_axis=0, tiled=True)
    arrived = arrived.reshape(lat_devices, lon_devices, slot_count, 2, group_width, lat_rows)
    arrived = arrived.transpose(2, 3, 1, 4, 0, 5).reshape(slot_count, 2 * channels, lat_total)
    spectra = jnp.einsum("slk,sqk->slq", associated, arrived, preferred_element_type=jnp.float32)
    scaled = apply_gain(spectra, spectral_gain).astype(jnp.bfloat16)
    mixing = complex_block(mix_weight)
    mixed_spec = jnp.dot(
        scaled.reshape(slot_count * degrees, 2 * channels),
        mixing,
        preferred_element_type=jnp.float32,
    ).astype(jnp.bfloat16)
    mixed_spec = mixed_spec.reshape(slot_count, degrees, 2 * channels)
    spectrum = mixed_spec.reshape(1, slot_count, degrees, 2, channels)
    returned = jnp.einsum(
        "slk,slq->sqk", associated, mixed_spec, preferred_element_type=jnp.float32
    ).astype(jnp.bfloat16)
    homeward = returned.reshape(slot_count, 2, lon_devices, group_width, lat_devices, lat_rows)
    homeward = homeward.transpose(4, 2, 0, 1, 3, 5).reshape(
        owners, slot_count, 2, group_width, lat_rows
    )
    landed = lax.all_to_all(homeward, ("lat", "lon"), split_axis=0, concat_axis=0, tiled=True)
    landed = landed.reshape(owners * slot_count, 2, group_width, lat_rows)
    factor = jnp.where(slot_orders == 0, 1.0, 2.0).astype(jnp.bfloat16)
    weighted = landed * factor[:, None, None, None]
    filtered = (
        jnp.einsum("spca,jsp->caj", weighted, fourier, preferred_element_type=jnp.float32)
        / float(lon_total)
    ).astype(jnp.bfloat16)
    filtered_home = lax.all_to_all(filtered, "lon", split_axis=2, concat_axis=0, tiled=True)
    blended = (
        channel_first.astype(jnp.float32)
        + jax.nn.gelu(filtered_home.astype(jnp.float32), approximate=False)
    ).astype(jnp.bfloat16)
    return (blended.transpose(1, 2, 0), spectrum)


def solution(mesh):
    placed = (P("lat", "lon", None), P(), P(), P(), P())
    return jax.shard_map(
        shards,
        mesh=mesh,
        in_specs=placed,
        out_specs=(P("lat", "lon", None), P(("lat", "lon"), None, None, None, None)),
        check_vma=False,
    )
```

profile of v0, /device:TPU:0, one launch (start us, length us, event | category | flops | bytes accessed | tf_op | source)
XLA Modules:
  0.0 756.0 jit_solution(6976904454536298545)
XLA Ops:
  19.2 23.0 %fusion.53 = (f32[1440,896,1]{1,0,2:T(8,128)}, f32[1440,896,1]{1,0,2:T(8,128)}) fusion(s32[896]{0:T(1024)S(1)} %select_reduce_fusion), kind=kLoop, calls=%fused_computation.246 | loop fusion | flops 12902400 | bytes 10325504 | tf_op jit(solution)/shard_map/cos | solution.py:19
  42.2 68.4 %all-to-all-done = bf16[256,90,90]{2,1,0:T(8,128)(2,1)} async-done(((bf16[256,90,90]{2,1,0:T(8,128)(2,1)}), bf16[256,90,90]{2,1,0:T(8,128)(2,1)}, u32[]{:S(2)}, u32[]{:S(2)}) %all-to-all-start) | async-done | bytes 4147232 | tf_op jit(solution)/shard_map/all_to_all | solution.py:121
  119.7 10.0 %reshape.1243 = bf16[16,90,1440,1]{2,1,0,3:T(8,128)(2,1)} reshape(bf16[16,90,16,90]{3,2,1,0:T(8,128)(2,1)} %copy.103) | data formatting | bytes 8294400 | tf_op jit(solution)/shard_map/all_to_all | solution.py:121
  129.7 15.7 %multiply_convert_fusion = bf16[896,2,16,90]{0,3,2,1:T(8,128)(2,1)} fusion(f32[90]{0:T(128)S(1)} %sine_multiply_fusion, bf16[16,90,1440,1]{2,1,0,3:T(8,128)(2,1)} %reshape.1243, f32[1440,896,1]{1,0,2:T(8,128)} %get-tuple-element.551, f32[1440,896,1]{1,0,2:T(8,128)} %get-tuple-element.550, f32[896]{0:T(1024)S(1)} %reshape.1239), kind=kOutput, calls=%fused_computation.220 | convolution fusion | flops 7444684800 | bytes 19634024 | tf_op jit(solution)/shard_map/caj,jsp->spca/dot_general | solution.py:119
  145.4 11.7 %copy.84 = bf16[896,2,16,90]{3,2,1,0:T(8,128)(2,1)} copy(bf16[896,2,16,90]{0,3,2,1:T(8,128)(2,1)} %multiply_convert_fusion) | data formatting | bytes 10321920 | tf_op jit(solution)/shard_map/convert_element_type | solution.py:126
  157.1 9.1 %all-to-all-start.1 = ((bf16[128,7,2,16,90]{4,3,2,1,0:T(8,128)(2,1)}), bf16[128,7,2,16,90]{4,3,2,1,0:T(8,128)(2,1)}, u32[]{:S(2)}, u32[]{:S(2)}) async-start(bf16[128,7,2,16,90]{4,3,2,1,0:T(8,128)(2,1)} %bitcast.357), calls=%async_computation.1 | async-start | bytes 14680064 | tf_op jit(solution)/shard_map/all_to_all | solution.py:128
  170.3 144.5 %while.24 = (s32[]{:T(128)}, f32[7,720]{1,0:T(8,128)S(1)}, f32[7,720]{1,0:T(8,128)S(1)}, f32[7,720]{1,0:T(8,128)S(1)}, bf16[7,720,720]{2,0,1:T(8,128)(2,1)}, /*i...) while((s32[]{:T(128)}, f32[7,720]{1,0:T(8,128)S(1)}, ...), condition=%wide.region_3.4_spmd.clone.clone, body=%wide.region_2.3_spmd.clone.clone.sunk | while | flops 2039413 | bytes 3433183 | solution.py:70
  314.8 12.8 %copy.89 = bf16[7,720,720]{1,2,0:T(8,128)(2,1)} copy(bf16[7,720,720]{2,0,1:T(8,128)(2,1)} %get-tuple-element.330) | data formatting | bytes 14515200 | tf_op jit(solution)/shard_map/while | solution.py:70
  329.0 14.5 %copy.114 = bf16[8,16,7,2,16,90]{5,0,4,1,3,2:T(8,128)(2,1)} copy(bf16[8,16,7,2,16,90]{5,4,3,2,1,0:T(8,128)(2,1)} %bitcast.12) | data formatting | bytes 10321920 | tf_op jit(solution)/shard_map/reshape | solution.py:129
  343.4 12.3 %reshape.1234 = bf16[7,512,720]{2,1,0:T(8,128)(2,1)} reshape(bf16[7,2,16,16,8,90]{5,4,3,2,1,0:T(8,128)(2,1)} %bitcast.359) | data formatting | bytes 10321920 | tf_op jit(solution)/shard_map/reshape | solution.py:130
  355.8 13.5 %fusion.78 = f32[7,720,512]{2,1,0:T(8,128)} fusion(bf16[7,720,720]{1,2,0:T(8,128)(2,1)} %copy.89, bf16[7,512,720]{2,1,0:T(8,128)(2,1)} %reshape.1234), kind=kOutput, calls=%fused_computation.311 | convolution fusion | flops 3715891200 | bytes 22740480 | tf_op jit(solution)/shard_map/slk,sqk->slq/dot_general | solution.py:131
  393.2 13.4 %reshape.1236 = bf16[7,2,16,16,8,90]{5,4,3,2,1,0:T(8,128)(2,1)} reshape(bf16[7,512,720]{2,1,0:T(8,128)(2,1)} %copy.90) | data formatting | bytes 10321920 | tf_op jit(solution)/shard_map/reshape | solution.py:144
  414.0 10.6 %all-to-all-start.2 = ((bf16[128,7,2,16,90]{4,3,2,1,0:T(8,128)(2,1)}), bf16[128,7,2,16,90]{4,3,2,1,0:T(8,128)(2,1)}, u32[]{:S(2)}, u32[]{:S(2)}) async-start(bf16[128,7,2,16,90]{4,3,2,1,0:T(8,128)(2,1)} %bitcast.358), calls=%async_computation.2 | async-start | bytes 14680064 | tf_op jit(solution)/shard_map/all_to_all | solution.py:148
  424.6 92.4 %all-to-all-done.2 = bf16[128,7,2,16,90]{4,3,2,1,0:T(8,128)(2,1)} async-done(((bf16[128,7,2,16,90]{4,3,2,1,0:T(8,128)(2,1)}), bf16[128,7,2,16,90]{4,3,2,1,0:T(8,128)(2,1)}, u32[]{:S(2)}, u32[]{:S(2)}) %all-to-all-start.2) | async-done | bytes 5160992 | tf_op jit(solution)/shard_map/all_to_all | solution.py:148
  522.5 20.8 %fusion.37 = bf16[16,90,1440]{2,1,0:T(8,128)(2,1)} fusion(bf16[896,2,16,90]{3,2,1,0:T(8,128)(2,1)S(1)} %bitcast_multiply_fusion.3, f32[1440,896,1]{1,0,2:T(8,128)} %get-tuple-element.551, f32[1440,896,1]{1,0,2:T(8,128)} %get-tuple-element.550, f32[896]{0:T(1024)S(1)} %reshape.1239), kind=kOutput, calls=%fused_computation.224 | convolution fusion | flops 7443671040 | bytes 19633664 | tf_op jit(solution)/shard_map/spca,jsp->caj/dot_general | solution.py:153
  564.5 11.3 %reshape_reshape.3 = bf16[1,7,720,2,256]{4,3,2,1,0:T(2,128)(2,1)} reshape(bf16[5040,512]{1,0:T(8,128)(2,1)} %copy-done) | data formatting | bytes 10321920 | tf_op jit(solution)/shard_map/reshape;reshape | solution.py:140
  575.8 64.9 %all-to-all-done.3 = bf16[16,90,1440]{1,0,2:T(8,128)(2,1)} async-done(((bf16[16,90,1440]{1,0,2:T(8,128)(2,1)}), bf16[16,90,1440]{1,0,2:T(8,128)(2,1)}, u32[]{:S(2)}, u32[]{:S(2)}) %all-to-all-start.3) | async-done | bytes 4147232 | tf_op jit(solution)/shard_map/all_to_all | solution.py:156
  640.7 9.3 %copy.94 = bf16[16,90,1440]{2,0,1:T(8,128)(2,1)} copy(bf16[16,90,1440]{1,0,2:T(8,128)(2,1)} %all-to-all-done.3) | data formatting | bytes 8294400 | tf_op jit(solution)/shard_map/all_to_all | solution.py:156
  650.0 10.8 %convert_multiply_fusion = (f32[16,90,1440]{2,0,1:T(8,128)}, f32[16,90,1440]{2,0,1:T(8,128)}) fusion(bf16[16,90,1440]{2,0,1:T(8,128)(2,1)} %copy.94), kind=kLoop, calls=%fused_computation.219 | loop fusion | flops 8294400 | bytes 20736000 | tf_op jit(solution)/shard_map/mul | solution.py:159
  660.8 15.1 %mul.2551 = f32[16,90,16,90]{3,2,0,1:T(8,128)} reshape(f32[16,90,1440]{2,0,1:T(8,128)} %get-tuple-element.544) | data formatting | bytes 16588800 | tf_op jit(solution)/shard_map/mul | solution.py:159
  675.9 14.3 %copy.95 = f32[16,16,90,90]{3,1,0,2:T(8,128)} copy(f32[16,16,90,90]{3,0,1,2:T(8,128)} %bitcast.355) | data formatting | bytes 16588800 | tf_op jit(solution)/shard_map/mul | solution.py:159
  690.2 15.4 %reshape.1241 = f32[16,90,16,90]{3,2,0,1:T(8,128)} reshape(f32[16,90,1440]{2,0,1:T(8,128)} %get-tuple-element.545) | data formatting | bytes 16588800 | tf_op jit(solution)/shard_map/mul | solution.py:159
  705.6 14.4 %copy.96 = f32[16,16,90,90]{3,1,0,2:T(8,128)} copy(f32[16,16,90,90]{3,0,1,2:T(8,128)} %bitcast.356) | data formatting | bytes 16588800 | tf_op jit(solution)/shard_map/mul | solution.py:159
  720.0 27.8 %fusion.21 = bf16[256,90,90]{2,0,1:T(8,128)(2,1)} fusion(f32[16,16,90,90]{3,1,0,2:T(8,128)} %copy.96, f32[16,16,90,90]{3,1,0,2:T(8,128)} %copy.95, bf16[90,90,256]{1,2,0:T(8,128)(2,1)S(1)} %bitcast.362), kind=kLoop, calls=%fused_computation.199 | loop fusion | flops 132710400 | bytes 24883200 | tf_op jit(solution)/shard_map/convert_element_type | solution.py:160
  (1136 shorter events, 226.3 us)
Async XLA Ops:
  9.1 8.4 %copy-start.4 = (s32[128]{0:T(128)S(1)}, s32[128]{0:T(128)}, u32[]{:S(2)}) copy-start(s32[128]{0:T(128)} %param.11) | copy-start | bytes 1540
  9.1 9.4 %copy-start.3 = (s32[720]{0:T(1024)S(1)}, s32[720]{0:T(1024)}, u32[]{:S(2)}) copy-start(s32[720]{0:T(1024)} %param.10) | copy-start | bytes 8644
  9.1 101.5 %all-to-all-start = ((bf16[256,90,90]{2,1,0:T(8,128)(2,1)}), bf16[256,90,90]{2,1,0:T(8,128)(2,1)}, u32[]{:S(2)}, u32[]{:S(2)}) async-start(bf16[256,90,90]{2,1,0:T(8,128)(2,1)} %copy.80), calls=%async_computation | async-start | bytes 12582912 | tf_op jit(solution)/shard_map/all_to_all | solution.py:121
  157.1 171.9 %all-to-all-start.1 = ((bf16[128,7,2,16,90]{4,3,2,1,0:T(8,128)(2,1)}), bf16[128,7,2,16,90]{4,3,2,1,0:T(8,128)(2,1)}, u32[]{:S(2)}, u32[]{:S(2)}) async-start(bf16[128,7,2,16,90]{4,3,2,1,0:T(8,128)(2,1)} %bitcast.357), calls=%async_computation.1 | async-start | bytes 14680064 | tf_op jit(solution)/shard_map/all_to_all | solution.py:128
  314.8 12.8 %copy-start.2 = (bf16[2,256,256]{2,1,0:T(8,128)(2,1)S(1)}, bf16[2,256,256]{2,1,0:T(8,128)(2,1)}, u32[]{:S(2)}) copy-start(bf16[2,256,256]{2,1,0:T(8,128)(2,1)} %param.9) | copy-start | bytes 786436
  314.8 12.9 %copy-start.1 = (f32[720,2,256]{2,1,0:T(2,128)S(1)}, f32[720,2,256]{2,1,0:T(2,128)}, u32[]{:S(2)}) copy-start(f32[720,2,256]{2,1,0:T(2,128)} %param.8) | copy-start | bytes 4423684
  369.2 10.3 %slice-start.2 = ((s8[7741440]{0:T(1024)(128)(4,1)}), s8[4194304]{0:T(1024)(128)(4,1)S(1)}, s32[]{:S(2)}) async-start(s8[7741440]{0:T(1024)(128)(4,1)} %bitcast.365), calls=%async_computation.6 | async-start | bytes 8388608
  374.2 5.3 slice-start.3
  377.3 2.2 copy-start
  414.0 103.0 %all-to-all-start.2 = ((bf16[128,7,2,16,90]{4,3,2,1,0:T(8,128)(2,1)}), bf16[128,7,2,16,90]{4,3,2,1,0:T(8,128)(2,1)}, u32[]{:S(2)}, u32[]{:S(2)}) async-start(bf16[128,7,2,16,90]{4,3,2,1,0:T(8,128)(2,1)} %bitcast.358), calls=%async_computation.2 | async-start | bytes 14680064 | tf_op jit(solution)/shard_map/all_to_all | solution.py:148
  551.9 88.8 %all-to-all-start.3 = ((bf16[16,90,1440]{1,0,2:T(8,128)(2,1)}), bf16[16,90,1440]{1,0,2:T(8,128)(2,1)}, u32[]{:S(2)}, u32[]{:S(2)}) async-start(bf16[16,90,1440]{1,0,2:T(8,128)(2,1)} %copy.93), calls=%async_computation.3 | async-start | bytes 11796480 | tf_op jit(solution)/shard_map/all_to_all | solution.py:156
  690.2 29.8 %slice-start = ((s8[5898240]{0:T(1024)(128)(4,1)}), s8[1703936]{0:T(1024)(128)(4,1)S(1)}, s32[]{:S(2)}) async-start(s8[5898240]{0:T(1024)(128)(4,1)} %bitcast.361), calls=%async_computation.4 | async-start | bytes 3407872
  705.6 14.4 %slice-start.1 = ((s8[5898240]{0:T(1024)(128)(4,1)}), s8[4194304]{0:T(1024)(128)(4,1)S(1)}, s32[]{:S(2)}) async-start(s8[5898240]{0:T(1024)(128)(4,1)} %bitcast.361), calls=%async_computation.5 | async-start | bytes 8388608
where the time goes:
time: 771 us; the launch traced here: 756 us
  local copies, waits for them, and re-layouts  251 us (33%)
  waiting for transfers between devices  226 us (29%)
  other arithmetic  170 us (22%)
  matrix products  58.9 us (8%)
  starting transfers between devices  32.8 us (4%)
  loops' own time  17.1 us (2%)
    all_to_all x1, waiting for transfers between devices, shards(): lax.all_to_all(homeward, ('lat', 'lon'), split_axis=0, concat_axis=0, til...  92.4 us
    while x675, other arithmetic  77.8 us
    all_to_all x1, waiting for transfers between devices, shards(): lax.all_to_all(channel_first, 'lon', split_axis=0, concat_axis=2, tiled=T...  68.4 us
    all_to_all x1, waiting for transfers between devices, shards(): lax.all_to_all(filtered, 'lon', split_axis=2, concat_axis=0, tiled=True)  64.9 us
    mul x4, local copies, waits for them, and re-layouts, shards(): jax.nn.gelu(filtered_home.astype(jnp.float32), approximate=False)  59.2 us
    dynamic_update_slice x45, local copies, waits for them, and re-layouts, fill_block(): lax.dynamic_update_slice(table, tile, (jnp.int32(0), first.astype(jnp.int...  31.2 us
    convert_element_type x1, other arithmetic, shards(): blended = (channel_first.astype(jnp.float32) + jax.nn.gelu(filtered_home....  27.8 us
    cos x1, other arithmetic, fourier_table(): stacked = jnp.stack([jnp.cos(angles), -jnp.sin(angles)], axis=2)  23 us
  transfers between devices with their start and end apart: 4, of which 3 were waited for; matrix products, arithmetic and copies ran while one was open for 25% of the time, Pallas kernels for 0%

commit v1 on v0

v1 whole, which is shorter than its diff:
```python
import functools
import math

import jax
import jax.numpy as jnp
from jax import lax
from jax.experimental import pallas as pl
from jax.experimental.pallas import tpu as pltpu
from jax.sharding import PartitionSpec as P

QUARTERS = 4
UNIT = 8
UNITS = 3
PAIRS = UNIT // 2
LON_PAD = 96
HALF = 64
LANES = 128
SLOTS = 7
LEVELS = 768
ROWS = 768
ROW_CHUNKS = ((0, 2), (2, 3))
SLOT_CHUNKS = ((0, 4), (4, 7))
VMEM = 56 * 1024 * 1024
LEVEL_BLOCK = 128
RESCALE = 8


def call(kernel, name, flops, moved, **kwargs):
    return pl.pallas_call(
        kernel,
        name=name,
        compiler_params=pltpu.CompilerParams(vmem_limit_bytes=VMEM),
        cost_estimate=pl.CostEstimate(flops=flops, bytes_accessed=moved, transcendentals=0),
        **kwargs,
    )


def low_half():
    return lax.broadcasted_iota(jnp.int32, (1, LANES), 1) < HALF


def swap(value):
    return pltpu.roll(value, HALF, value.ndim - 1)


def join_low(first, second):
    return jnp.where(low_half(), first, swap(second))


def join_high(first, second):
    return jnp.where(low_half(), swap(first), second)


def pack_kernel(unit_first, band_rows, fields_ref, out_ref):
    lon_cols = fields_ref.shape[1]
    base = (pl.program_id(0) * UNITS + unit_first + pl.program_id(1)) * UNIT
    out_ref[...] = jnp.zeros_like(out_ref)
    for pair in range(PAIRS):
        first = fields_ref[2 * pair].astype(jnp.float32)
        second = fields_ref[2 * pair + 1].astype(jnp.float32)
        first = jnp.where(base + 2 * pair < band_rows, first, 0.0)
        second = jnp.where(base + 2 * pair + 1 < band_rows, second, 0.0)
        for tile in range(2):
            lanes = slice(tile * LANES, (tile + 1) * LANES)
            one, two = first[:, lanes], second[:, lanes]
            out_ref[0, 2 * tile, pair, :lon_cols] = join_low(one, two).astype(jnp.bfloat16)
            out_ref[0, 2 * tile + 1, pair, :lon_cols] = join_high(one, two).astype(jnp.bfloat16)


def pack(fields, chunk):
    band_rows, lon_cols, channels = fields.shape
    first, last = chunk
    count = last - first
    out = call(
        functools.partial(pack_kernel, first, band_rows),
        "pack",
        0,
        2 * 2 * count * UNIT * QUARTERS * LON_PAD * channels,
        grid=(QUARTERS, count),
        in_specs=[
            pl.BlockSpec((UNIT, lon_cols, channels), lambda q, u: (q * UNITS + first + u, 0, 0))
        ],
        out_specs=pl.BlockSpec(
            (1, QUARTERS, PAIRS, LON_PAD, LANES), lambda q, u: (q, 0, u, 0, 0)
        ),
        out_shape=jax.ShapeDtypeStruct(
            (QUARTERS, QUARTERS, count * PAIRS, LON_PAD, LANES), jnp.bfloat16
        ),
    )(fields)
    return out.reshape(QUARTERS * QUARTERS, count * PAIRS, LON_PAD, LANES)


def forward_kernel(chunk_count, has_alias, *refs):
    arrived_ref, table_ref, weight_ref = refs[:3]
    refs = refs[3 + (chunk_count if has_alias else 0) :]
    out_refs, matrix, turned = refs[:chunk_count], refs[chunk_count], refs[chunk_count + 1]
    sources = arrived_ref.shape[0]
    for pair in range(PAIRS):
        matrix[:, pair * LANES : (pair + 1) * LANES] = arrived_ref[:, pair].reshape(
            sources * LON_PAD, LANES
        )
    weights = weight_ref[0]
    owners = table_ref.shape[2]

    def one_slot(slot, out_ref, place):
        table = table_ref[slot].reshape(2 * owners, sources * LON_PAD)
        summed = jnp.dot(table, matrix[...], preferred_element_type=jnp.float32) * weights
        for pair in range(PAIRS):
            real = summed[:owners, pair * LANES : (pair + 1) * LANES]
            imag = summed[owners:, pair * LANES : (pair + 1) * LANES]
            turned[pl.ds(2 * pair, owners, stride=UNIT), :] = join_low(real, imag)
            turned[pl.ds(2 * pair + 1, owners, stride=UNIT), :] = join_high(real, imag)
        out_ref[:, place, 0] = turned[...].reshape(owners, UNIT, LANES).astype(jnp.bfloat16)

    for out_ref, (start, stop) in zip(out_refs, SLOT_CHUNKS):

        def step(place, carry, out_ref=out_ref, start=start):
            one_slot(start + place, out_ref, place)
            return carry

        lax.fori_loop(0, stop - start, step, 0)


def forward(arrived, table, weights, chunk, buffers):
    first, last = chunk
    count = last - first
    sources = arrived.shape[0]
    owners = table.shape[2]
    shapes = [
        jax.ShapeDtypeStruct((owners, stop - start, UNITS, UNIT, LANES), jnp.bfloat16)
        for start, stop in SLOT_CHUNKS
    ]
    has_alias = buffers is not None
    operands = [arrived, table, weights] + (list(buffers) if has_alias else [])
    return call(
        functools.partial(forward_kernel, len(shapes), has_alias),
        "forward",
        2 * count * table.size * PAIRS * LANES,
        2 * (arrived.size + table.size),
        grid=(count,),
        in_specs=[
            pl.BlockSpec((sources, PAIRS, LON_PAD, LANES), lambda u: (0, u, 0, 0)),
            pl.BlockSpec(table.shape, lambda u: (0, 0, 0, 0)),
            pl.BlockSpec((1, 1, PAIRS * LANES), lambda u: (first + u, 0, 0)),
        ]
        + ([pl.BlockSpec(memory_space=pl.ANY)] * len(shapes) if has_alias else []),
        out_specs=[
            pl.BlockSpec((owners, s.shape[1], 1, UNIT, LANES), lambda u: (0, 0, first + u, 0, 0))
            for s in shapes
        ],
        out_shape=shapes,
        scratch_shapes=[
            pltpu.VMEM((sources * LON_PAD, PAIRS * LANES), jnp.bfloat16),
            pltpu.VMEM((owners * UNIT, LANES), jnp.float32),
        ],
        input_output_aliases={3 + i: i for i in range(len(shapes))} if has_alias else {},
    )(*operands)


def middle_kernel(has_alias, *refs):
    arrived_ref, table_ref, turned_ref, gain_ref, cross_ref, mixing_ref = refs[:6]
    spectrum_ref, out_ref = refs[7:] if has_alias else refs[6:]
    degrees = spectrum_ref.shape[1]
    arrived = arrived_ref[:, 0].astype(jnp.float32)
    groups = arrived.shape[0] // QUARTERS
    arrived = arrived.reshape(groups, QUARTERS, UNITS * UNIT, LANES)
    columns = jnp.concatenate(
        [
            arrived[:, quarter].reshape(ROWS, LANES).astype(jnp.bfloat16)
            for quarter in range(QUARTERS)
        ],
        axis=1,
    )
    spectra = jnp.dot(table_ref[0], columns, preferred_element_type=jnp.float32)
    parts = []
    for quarter in range(QUARTERS):
        lanes = slice(quarter * LANES, (quarter + 1) * LANES)
        piece = spectra[:, lanes]
        parts.append(
            (gain_ref[:, lanes] * piece + cross_ref[:, lanes] * swap(piece)).astype(jnp.bfloat16)
        )
    scaled = jnp.concatenate(parts, axis=1)
    mixed = jnp.dot(scaled, mixing_ref[...], preferred_element_type=jnp.float32)
    pieces = [mixed[:, q * LANES : (q + 1) * LANES] for q in range(QUARTERS)]
    for tile in range(2):
        one, two = pieces[2 * tile][:degrees], pieces[2 * tile + 1][:degrees]
        lanes = slice(tile * LANES, (tile + 1) * LANES)
        spectrum_ref[0, :, lanes] = join_low(one, two).astype(jnp.bfloat16)
        lanes = slice((2 + tile) * LANES, (3 + tile) * LANES)
        spectrum_ref[0, :, lanes] = join_high(one, two).astype(jnp.bfloat16)
    returned = jnp.dot(
        turned_ref[0], mixed.astype(jnp.bfloat16), preferred_element_type=jnp.float32
    )
    for quarter in range(QUARTERS):
        piece = returned[:, quarter * LANES : (quarter + 1) * LANES]
        out_ref[:, quarter, 0] = piece.reshape(groups, UNITS, UNIT, LANES).astype(jnp.bfloat16)


def middle(arrived, table, turned, gain, cross, mixing, slots, degrees, spectrum):
    start, stop = slots
    owners = arrived.shape[0]
    groups = owners // QUARTERS
    width = mixing.shape[0]
    has_alias = spectrum is not None
    operands = [arrived, table, turned, gain, cross, mixing] + ([spectrum] if has_alias else [])
    spectrum, out = call(
        functools.partial(middle_kernel, has_alias),
        "middle",
        2 * (stop - start) * LEVELS * width * (2 * ROWS + width),
        (stop - start) * (4 * LEVELS * ROWS + 6 * LEVELS * width),
        grid=(stop - start,),
        in_specs=[
            pl.BlockSpec((owners, 1, UNITS, UNIT, LANES), lambda s: (0, s, 0, 0, 0)),
            pl.BlockSpec((1, LEVELS, ROWS), lambda s: (start + s, 0, 0)),
            pl.BlockSpec((1, ROWS, LEVELS), lambda s: (start + s, 0, 0)),
            pl.BlockSpec(gain.shape, lambda s: (0, 0)),
            pl.BlockSpec(cross.shape, lambda s: (0, 0)),
            pl.BlockSpec(mixing.shape, lambda s: (0, 0)),
        ]
        + ([pl.BlockSpec(memory_space=pl.ANY)] if has_alias else []),
        out_specs=[
            pl.BlockSpec((1, degrees, width), lambda s: (start + s, 0, 0)),
            pl.BlockSpec((groups, QUARTERS, 1, UNITS, UNIT, LANES), lambda s: (0, 0, s, 0, 0, 0)),
        ],
        out_shape=[
            jax.ShapeDtypeStruct((SLOTS, degrees, width), jnp.bfloat16),
            jax.ShapeDtypeStruct(
                (groups, QUARTERS, stop - start, UNITS, UNIT, LANES), jnp.bfloat16
            ),
        ],
        input_output_aliases={6: 0} if has_alias else {},
    )(*operands)
    return spectrum, out.reshape(owners, stop - start, UNITS, UNIT, LANES)


def inverse_kernel(scale, chunk_count, *refs):
    arrived_refs, table_ref, out_ref = refs[:chunk_count], refs[chunk_count], refs[chunk_count + 1]
    wide, matrix = refs[chunk_count + 2], refs[chunk_count + 3]
    owners = arrived_refs[0].shape[0]
    for arrived_ref, (start, stop) in zip(arrived_refs, SLOT_CHUNKS):

        def one_slot(place, carry, arrived_ref=arrived_ref, start=start):
            wide[...] = arrived_ref[:, place, 0].astype(jnp.float32).reshape(owners * UNIT, LANES)
            row = pl.multiple_of((start + place) * 2 * owners, 2 * owners)
            for pair in range(PAIRS):
                one = wide[pl.ds(2 * pair, owners, stride=UNIT), :]
                two = wide[pl.ds(2 * pair + 1, owners, stride=UNIT), :]
                lanes = slice(pair * LANES, (pair + 1) * LANES)
                matrix[pl.ds(row, owners), lanes] = join_low(one, two).astype(jnp.bfloat16)
                matrix[pl.ds(row + owners, owners), lanes] = join_high(one, two).astype(
                    jnp.bfloat16
                )
            return carry

        lax.fori_loop(0, stop - start, one_slot, 0)
    blocks = 4
    rows = blocks * LON_PAD

    def some_columns(step, carry):
        row = pl.multiple_of(step * rows, rows)
        summed = jnp.dot(
            table_ref[pl.ds(row, rows), :], matrix[...], preferred_element_type=jnp.float32
        )
        summed = (summed * scale).astype(jnp.bfloat16)
        for pair in range(PAIRS):
            out_ref[pl.ds(step * blocks, blocks), pair] = summed[
                :, pair * LANES : (pair + 1) * LANES
            ].reshape(blocks, LON_PAD, LANES)
        return carry

    lax.fori_loop(0, table_ref.shape[0] // rows, some_columns, 0)


def inverse(arrived, table, chunk, lon_total):
    first, last = chunk
    count = last - first
    owners = arrived[0].shape[0]
    targets = table.shape[0] // LON_PAD
    return call(
        functools.partial(inverse_kernel, 1.0 / lon_total, len(arrived)),
        "inverse",
        2 * count * table.size * PAIRS * LANES,
        2 * 2 * table.size,
        grid=(count,),
        in_specs=[
            pl.BlockSpec((owners, a.shape[1], 1, UNIT, LANES), lambda u: (0, 0, first + u, 0, 0))
            for a in arrived
        ]
        + [pl.BlockSpec(table.shape, lambda u: (0, 0))],
        out_specs=pl.BlockSpec((targets, PAIRS, LON_PAD, LANES), lambda u: (0, u, 0, 0)),
        out_shape=jax.ShapeDtypeStruct((targets, count * PAIRS, LON_PAD, LANES), jnp.bfloat16),
        scratch_shapes=[
            pltpu.VMEM((owners * UNIT, LANES), jnp.float32),
            pltpu.VMEM((table.shape[1], PAIRS * LANES), jnp.bfloat16),
        ],
    )(*arrived, table)


def blend_kernel(has_alias, *refs):
    arrived_ref, fields_ref = refs[:2]
    out_ref = refs[-1]
    lon_cols = fields_ref.shape[1]

    def gelu(value):
        return 0.5 * value * (1.0 + lax.erf(value * math.sqrt(0.5)))

    for pair in range(PAIRS):
        for tile in range(2):
            lanes = slice(tile * LANES, (tile + 1) * LANES)
            one = gelu(arrived_ref[0, 2 * tile, pair, :lon_cols].astype(jnp.float32))
            two = gelu(arrived_ref[0, 2 * tile + 1, pair, :lon_cols].astype(jnp.float32))
            for row, value in ((2 * pair, join_low(one, two)), (2 * pair + 1, join_high(one, two))):
                held = fields_ref[row, :, lanes].astype(jnp.float32)
                out_ref[row, :, lanes] = (held + value).astype(jnp.bfloat16)


def blend(arrived, fields, chunk, buffer):
    first, last = chunk
    count = last - first
    band_rows, lon_cols, channels = fields.shape
    has_alias = buffer is not None
    arrived = arrived.reshape(QUARTERS, QUARTERS, count * PAIRS, LON_PAD, LANES)
    held = pl.BlockSpec((UNIT, lon_cols, channels), lambda q, u: (q * UNITS + first + u, 0, 0))
    return call(
        functools.partial(blend_kernel, has_alias),
        "blend",
        60 * count * UNIT * QUARTERS * lon_cols * channels,
        6 * count * UNIT * QUARTERS * lon_cols * channels,
        grid=(QUARTERS, count),
        in_specs=[
            pl.BlockSpec((1, QUARTERS, PAIRS, LON_PAD, LANES), lambda q, u: (q, 0, u, 0, 0)),
            held,
        ]
        + ([pl.BlockSpec(memory_space=pl.ANY)] if has_alias else []),
        out_specs=held,
        out_shape=jax.ShapeDtypeStruct(fields.shape, fields.dtype),
        input_output_aliases={2: 0} if has_alias else {},
    )(arrived, fields, *([buffer] if has_alias else []))


def legendre_kernel(degrees, order_ref, start_ref, lat_ref, out_ref, state, rows):
    tiles = ROWS // LANES
    order = order_ref[...]

    @pl.when(pl.program_id(0) == 0)
    def _():
        for tile in range(tiles):
            lanes = slice(tile * LANES, (tile + 1) * LANES)
            state[0, :, lanes] = jnp.zeros_like(order)
            state[1, :, lanes] = jnp.ones_like(order)
            state[2, :, lanes] = start_ref[...] + order * jnp.log(lat_ref[1:2, lanes])

    def pieces(index):
        return tuple(state[index, :, t * LANES : (t + 1) * LANES] for t in range(tiles))

    cosines = tuple(lat_ref[0:1, t * LANES : (t + 1) * LANES] for t in range(tiles))
    first = pl.program_id(0) * LEVEL_BLOCK

    def group(index, carry):
        previous, current, log_scale = [list(part) for part in carry]
        halves = []
        for tile in range(tiles):
            largest = jnp.maximum(jnp.abs(previous[tile]), jnp.abs(current[tile]))
            shrink = 1.0 / largest
            previous[tile] = previous[tile] * shrink
            current[tile] = current[tile] * shrink
            log_scale[tile] = log_scale[tile] + jnp.log(largest)
            halves.append(jnp.exp(0.5 * log_scale[tile]))
        for inner in range(RESCALE):
            level = (first + index * RESCALE + inner).astype(jnp.float32)
            square = (level - 1.0) * (level - 1.0)
            upper = jnp.sqrt(
                jnp.maximum(4.0 * level * level - 1.0, 0.0)
                / jnp.maximum(level * level - order * order, 1.0)
            )
            lower = jnp.sqrt(
                jnp.maximum(square - order * order, 0.0) / jnp.maximum(4.0 * square - 1.0, 1.0)
            )
            moving = level > order
            shown = jnp.logical_and(level >= order, level < degrees)
            row = pl.multiple_of((index * RESCALE + inner) * 8, 8)
            for tile in range(tiles):
                advanced = upper * (cosines[tile] * current[tile] - lower * previous[tile])
                previous[tile] = jnp.where(moving, current[tile], previous[tile])
                current[tile] = jnp.where(moving, advanced, current[tile])
                value = (current[tile] * halves[tile]) * halves[tile]
                rows[tile, pl.ds(row, 8), :] = jnp.where(shown, value, 0.0)
        return tuple(previous), tuple(current), tuple(log_scale)

    done = lax.fori_loop(
        0, LEVEL_BLOCK // RESCALE, group, (pieces(0), pieces(1), pieces(2))
    )
    for index in range(3):
        for tile in range(tiles):
            state[index, :, tile * LANES : (tile + 1) * LANES] = done[index][tile]
    for slot in range(SLOTS):
        for tile in range(tiles):
            out_ref[slot, :, tile * LANES : (tile + 1) * LANES] = rows[
                tile, pl.ds(slot, LEVEL_BLOCK, stride=8), :
            ].astype(jnp.bfloat16)


def legendre(orders, colatitude, degrees):
    order_col = orders.astype(jnp.float32)
    half_gamma = 0.5 * math.log(math.pi) - math.log(2.0)
    log_start = -0.5 * math.log(2.0) + 0.5 * (
        lax.lgamma(order_col + 1.5) - half_gamma - lax.lgamma(order_col + 1.0)
    )
    widen = lambda a: jnp.broadcast_to(jnp.pad(a, (0, 8 - SLOTS))[:, None], (8, LANES))
    lat = jnp.stack([jnp.cos(colatitude), jnp.sin(colatitude)])
    return call(
        functools.partial(legendre_kernel, degrees),
        "legendre",
        30 * LEVELS * 8 * ROWS,
        2 * SLOTS * LEVELS * ROWS,
        grid=(LEVELS // LEVEL_BLOCK,),
        in_specs=[
            pl.BlockSpec((8, LANES), lambda i: (0, 0)),
            pl.BlockSpec((8, LANES), lambda i: (0, 0)),
            pl.BlockSpec((2, ROWS), lambda i: (0, 0)),
        ],
        out_specs=pl.BlockSpec((SLOTS, LEVEL_BLOCK, ROWS), lambda i: (0, i, 0)),
        out_shape=jax.ShapeDtypeStruct((SLOTS, LEVELS, ROWS), jnp.bfloat16),
        scratch_shapes=[
            pltpu.VMEM((3, 8, ROWS), jnp.float32),
            pltpu.VMEM((ROWS // LANES, LEVEL_BLOCK * 8, LANES), jnp.float32),
        ],
    )(widen(order_col), widen(log_start), lat)


def fourier_tables(orders, live, lon_devices, lon_cols):
    lon_total = lon_devices * lon_cols
    place = jnp.arange(lon_devices * LON_PAD, dtype=jnp.int32)
    block, inside = place // LON_PAD, place % LON_PAD
    longitude = (block * lon_cols + inside).astype(jnp.float32)
    product = orders.astype(jnp.float32)[:, :, None] * longitude
    wrapped = product - lon_total * jnp.floor(product * (1.0 / lon_total))
    wrapped = jnp.where(wrapped < 0, wrapped + lon_total, wrapped)
    wrapped = jnp.where(wrapped >= lon_total, wrapped - lon_total, wrapped)
    angles = wrapped * (2.0 * math.pi / lon_total)
    mask = live[:, :, None] * (inside < lon_cols).astype(jnp.float32)
    return jnp.stack([jnp.cos(angles) * mask, -jnp.sin(angles) * mask], axis=1).astype(jnp.bfloat16)


def regroup(array, axis):
    shape = array.shape
    split = shape[:axis] + (2, QUARTERS, HALF) + shape[axis + 1 :]
    return jnp.swapaxes(array.reshape(split), axis, axis + 1).reshape(shape)


def complex_block(mix_weight):
    top_half = jnp.concatenate([mix_weight[0], mix_weight[1]], axis=1)
    bottom_half = jnp.concatenate([-mix_weight[1], mix_weight[0]], axis=1)
    return jnp.concatenate([top_half, bottom_half], axis=0)


def exchange(array, axes):
    return lax.all_to_all(array, axes, split_axis=0, concat_axis=0, tiled=True)


def shards(fields, spectral_gain, mix_weight, column_list, column_counts):
    band_rows, lon_cols, channels = fields.shape
    lat_devices = lax.axis_size("lat")
    lon_devices = lax.axis_size("lon")
    owners = lat_devices * lon_devices
    lat_total = band_rows * lat_devices
    lon_total = lon_cols * lon_devices
    degrees = spectral_gain.shape[0]
    mode_count = column_list.shape[0]

    gathered = [exchange(pack(fields, chunk), "lon") for chunk in ROW_CHUNKS]

    run_ends = jnp.cumsum(column_counts)
    starts = run_ends - column_counts
    offsets = jnp.arange(SLOTS, dtype=jnp.int32)
    positions = jnp.minimum(starts[None, :] + offsets[:, None], mode_count - 1)
    live = (offsets[:, None] < column_counts[None, :]).astype(jnp.float32)
    matches = positions[:, :, None] == jnp.arange(mode_count, dtype=jnp.int32)
    slot_orders = jnp.sum(jnp.where(matches, column_list, 0), axis=2)
    table = fourier_tables(slot_orders, live, lon_devices, lon_cols)
    factor = jnp.where(slot_orders == 0, 1.0, 2.0).astype(jnp.bfloat16)
    back_table = (table * factor[:, None, :, None]).reshape(
        SLOTS * 2 * owners, lon_devices * LON_PAD
    ).T

    owner_index = lax.axis_index(("lat", "lon"))
    own_orders = lax.dynamic_slice_in_dim(slot_orders, owner_index, 1, axis=1)[:, 0]
    padded = jnp.arange(ROWS, dtype=jnp.int32)
    band, inside = padded // (ROWS // lat_devices), padded % (ROWS // lat_devices)
    row = (band * band_rows + jnp.minimum(inside, band_rows - 1)).astype(jnp.float32)
    associated = legendre(own_orders, math.pi * (row + 0.5) / lat_total, degrees)
    turned = jnp.swapaxes(associated, 1, 2)

    group = lax.axis_index("lon") // QUARTERS
    mine = jnp.arange(UNITS * UNIT, dtype=jnp.int32) + group * (UNITS * UNIT)
    mine = (lax.axis_index("lat") * band_rows + mine).astype(jnp.float32)
    weights = math.pi / lat_total * jnp.sin(math.pi * (mine + 0.5) / lat_total)
    weights = jnp.repeat(weights.reshape(UNITS, 1, UNIT), HALF, axis=2)

    real, imag = spectral_gain[:, 0], spectral_gain[:, 1]
    fill = ((0, LEVELS - degrees), (0, 0))
    gain = jnp.pad(regroup(jnp.concatenate([real, real], axis=1), 1), fill)
    cross = jnp.pad(regroup(jnp.concatenate([-imag, imag], axis=1), 1), fill)
    mixing = regroup(regroup(complex_block(mix_weight), 0), 1)

    sends = None
    for chunk, arrived in zip(ROW_CHUNKS, gathered):
        sends = forward(arrived, table, weights, chunk, sends)
    arrived = [exchange(send, ("lat", "lon")) for send in sends]
    spectrum, landed = None, []
    for slots, part in zip(SLOT_CHUNKS, arrived):
        spectrum, send = middle(
            part, associated, turned, gain, cross, mixing, slots, degrees, spectrum
        )
        landed.append(exchange(send, ("lat", "lon")))
    blended = None
    for chunk in ROW_CHUNKS:
        home = exchange(inverse(landed, back_table, chunk, lon_total), "lon")
        blended = blend(home, fields, chunk, blended)
    return blended, spectrum.reshape(1, SLOTS, degrees, 2, channels)


def solution(mesh):
    placed = (P("lat", "lon", None), P(), P(), P(), P())
    return jax.shard_map(
        shards,
        mesh=mesh,
        in_specs=placed,
        out_specs=(P("lat", "lon", None), P(("lat", "lon"), None, None, None, None)),
        check_vma=False,
    )
```

time: 771 us -> 448 us (0.58); the launches traced: 756 us -> 446 us
  local copies, waits for them, and re-layouts: 251 us -> 68.7 us
  other arithmetic: 170 us -> 33.4 us
  waiting for transfers between devices: 226 us -> 110 us
  Pallas kernels: 0 us -> 108 us
  blocking collectives: 0 us -> 92.6 us
  matrix products: 58.9 us -> 0 us
  loops' own time: 17.1 us -> 0 us
    all_to_all x4 -> x6, waiting for transfers between devices: 226 us -> 110 us  [exchange(): return lax.all_to_all(array, axes, split_axis=0, concat_axis=0, tiled=True)]
    pallas_call x0 -> x11, Pallas kernels: none -> 108 us  [the longest x2 24.7 us: forward(): call(functools.partial(forward_kernel, len(shapes), has_alias), 'forward'...]
    all_to_all x0 -> x2, blocking collectives: none -> 92.6 us  [exchange(): return lax.all_to_all(array, axes, split_axis=0, concat_axis=0, tiled=True)]
    while x675 -> x0, other arithmetic: 77.8 us -> none
    mul x5 -> x2, local copies, waits for them, and re-layouts: 59.3 us -> 0.02 us  [shards(): table * factor[:, None, :, None]]
    dot_general x5 -> x0, matrix products: 58.9 us -> none  [the longest x1 20.8 us: shards(): jnp.einsum('spca,jsp->caj', weighted, fourier, preferred_element_type=jnp...]
    dynamic_update_slice x45 -> x0, local copies, waits for them, and re-layouts: 31.2 us -> none  [fill_block(): lax.dynamic_update_slice(table, tile, (jnp.int32(0), first.astype(jnp.int...]
    all_to_all x3 -> x0, local copies, waits for them, and re-layouts: 28.4 us -> none  [the longest x2 19.1 us: shards(): lax.all_to_all(channel_first, 'lon', split_axis=0, concat_axis=2, tiled=T...]
  transfers between devices with their start and end apart: 4 -> 6, of which waited for: 3 -> 4; matrix products, arithmetic and copies ran while one was open for 25% -> 22% of each run, Pallas kernels for 0% -> 14%
where the time goes in v1:
time: 448 us; the launch traced here: 446 us
  waiting for transfers between devices  110 us (25%)
  Pallas kernels  108 us (24%)
  blocking collectives  92.6 us (21%)
  local copies, waits for them, and re-layouts  68.7 us (15%)
  other arithmetic  33.4 us (7%)
  starting transfers between devices  31.4 us (7%)
    all_to_all x6, waiting for transfers between devices, exchange(): return lax.all_to_all(array, axes, split_axis=0, concat_axis=0, tiled=True)  110 us
    all_to_all x2, blocking collectives, exchange(): return lax.all_to_all(array, axes, split_axis=0, concat_axis=0, tiled=True)  92.6 us
    all_to_all x6, starting transfers between devices, exchange(): return lax.all_to_all(array, axes, split_axis=0, concat_axis=0, tiled=True)  31.4 us
    pallas_call x2, Pallas kernels, forward(): call(functools.partial(forward_kernel, len(shapes), has_alias), 'forward'...  24.7 us
    pallas_call x2, Pallas kernels, inverse(): call(functools.partial(inverse_kernel, 1.0 / lon_total, len(arrived)), 'i...  23.6 us
    mul x1, other arithmetic, fourier_tables(): jnp.cos(angles) * mask  23.1 us
    pallas_call x2, Pallas kernels, middle(): call(functools.partial(middle_kernel, has_alias), 'middle', 2 * (stop - s...  21.3 us
    pallas_call x1, Pallas kernels, legendre(): call(functools.partial(legendre_kernel, degrees), 'legendre', 30 * LEVELS...  16.2 us
  transfers between devices with their start and end apart: 6, of which 4 were waited for; matrix products, arithmetic and copies ran while one was open for 22% of the time, Pallas kernels for 14%

profile of v1, /device:TPU:0, one launch (start us, length us, event | category | flops | bytes accessed | tf_op | source)
XLA Modules:
  0.0 445.6 jit_solution(7487618977434756248)
XLA Ops:
  0.6 6.8 %pack.3 = bf16[4,4,8,96,128]{4,3,2,1,0:T(8,128)(2,1)} custom-call(bf16[90,90,256]{2,1,0:T(8,128)(2,1)} %refs_1_.3), custom_call_target="tpu_custom_call" | custom-call | bytes 6291456 | tf_op jit(solution)/shard_map/pack/pallas_call | solution.py:74
  7.4 8.1 %all-to-all-start.1 = ((bf16[16,8,96,128]{3,2,1,0:T(8,128)(2,1)}), bf16[16,8,96,128]{3,2,1,0:T(8,128)(2,1)S(1)}, u32[]{:S(2)}, u32[]{:S(2)}) async-start(bf16[16,8,96,128]{3,2,1,0:T(8,128)(2,1)} %bitcast.36), calls=%async_computation.1 | async-start | bytes 6291456 | tf_op jit(solution)/shard_map/all_to_all | solution.py:458
  21.2 41.9 %all-to-all-done.1.refs_0_ = bf16[16,8,96,128]{3,2,1,0:T(8,128)(2,1)S(1)} async-done(((bf16[16,8,96,128]{3,2,1,0:T(8,128)(2,1)}), bf16[16,8,96,128]{3,2,1,0:T(8,128)(2,1)S(1)}, u32[]{:S(2)}, u32[]{:S(2)}) %all-to-all-start.1) | async-done | bytes 3145760 | tf_op jit(solution)/shard_map/all_to_all | solution.py:458
  64.7 4.4 all-to-all-start
  69.1 23.1 %multiply_multiply_fusion.1 = (bf16[7,1,128,1536]{3,2,1,0:T(8,128)(2,1)S(1)}, bf16[7,1,128,1536]{3,2,1,0:T(8,128)(2,1)S(1)}) fusion(f32[1536]{0:T(1024)S(1)} %fusion.14, f32[7,128]{1,0:T(8,128)S(1)} %fusion.15, f32[1536]{0:T(1024)S(1)} %fusion.11, f32[7,128]{1,0:T(8,128)S(1)} %convert_element_type.73), kind=kLoop, calls=%fused_computation.4 | loop fusion | flops 24772608 | bytes 5524480 | tf_op jit(solution)/shard_map/mul | solution.py:442
  95.1 15.3 %forward.2 = (bf16[128,4,3,8,128]{4,3,2,1,0:T(8,128)(2,1)}, bf16[128,3,3,8,128]{4,3,2,1,0:T(8,128)(2,1)}) custom-call(bf16[16,8,96,128]{3,2,1,0:T(8,128)(2,1)} %copy-done.4, bf16[7,2,128,1536]{3,2,1,0:T(8,128)(2,1)} %maximum_convert_fusion.refs_1_, f32[3,1,512]{2,1,0:T(1,128)} %broadcast_in_dim.27.refs_2_), custom_call_target="tpu_custom_call" | custom-call | flops 5637144576 | bytes 8650752 | tf_op jit(solution)/shard_map/forward/pallas_call | solution.py:135
  111.5 9.4 %forward.3 = (bf16[128,4,3,8,128]{4,3,2,1,0:T(8,128)(2,1)}, bf16[128,3,3,8,128]{4,3,2,1,0:T(8,128)(2,1)}) custom-call(bf16[16,4,96,128]{3,2,1,0:T(8,128)(2,1)} %copy-done.3, bf16[7,2,128,1536]{3,2,1,0:T(8,128)(2,1)} %maximum_convert_fusion.refs_1_, f32[3,1,512]{2,1,0:T(1,128)} %broadcast_in_dim.27.refs_2_, ...), custom_call_target="tpu_custom_call", output_to_operand_aliasing={{0}: (3, {}), {1}: (4, {})} | custom-call | flops 2818572288 | bytes 7077888 | tf_op jit(solution)/shard_map/forward/pallas_call | solution.py:135
  120.9 50.6 %all_to_all.40.refs_0_ = bf16[128,4,3,8,128]{4,3,2,1,0:T(8,128)(2,1)} all-to-all(bf16[128,4,3,8,128]{4,3,2,1,0:T(8,128)(2,1)} %get-tuple-element.12), channel_id=1, replica_groups=mesh['lat'=8,'lon'=16] {'lat','lon'}, dimensions={0} | all-to-all | bytes 6291456 | tf_op jit(solution)/shard_map/all_to_all | solution.py:458
  171.5 5.5 %all-to-all-start.4 = ((bf16[128,3,3,8,128]{4,3,2,1,0:T(8,128)(2,1)}), bf16[128,3,3,8,128]{4,3,2,1,0:T(8,128)(2,1)S(1)}, u32[]{:S(2)}, u32[]{:S(2)}) async-start(bf16[128,3,3,8,128]{4,3,2,1,0:T(8,128)(2,1)} %get-tuple-element.14), calls=%async_computation.4 | async-start | bytes 4718592 | tf_op jit(solution)/shard_map/all_to_all | solution.py:458
  208.9 16.2 %legendre.1.refs_1_ = bf16[7,768,768]{2,1,0:T(8,128)(2,1)} custom-call(f32[8,128]{1,0:T(8,128)} %broadcast_in_dim.48.order_ref, f32[8,128]{1,0:T(8,128)} %broadcast_in_dim.49.start_ref, f32[2,768]{1,0:T(2,128)} %pad_maximum_fusion.lat_ref), custom_call_target="tpu_custom_call" | custom-call | flops 141557760 | bytes 8257536 | tf_op jit(solution)/shard_map/legendre/pallas_call | solution.py:411
  225.1 11.8 %copy.49 = bf16[7,768,768]{1,2,0:T(8,128)(2,1)} copy(bf16[7,768,768]{2,1,0:T(8,128)(2,1)} %legendre.1.refs_1_) | data formatting | bytes 16515072 | tf_op jit(solution)/shard_map/legendre/pallas_call | solution.py:411
  236.8 11.6 %middle.2 = (bf16[7,720,512]{2,1,0:T(8,128)(2,1)}, bf16[32,4,4,3,8,128]{5,4,3,2,1,0:T(8,128)(2,1)}) custom-call(bf16[128,4,3,8,128]{4,3,2,1,0:T(8,128)(2,1)} %all_to_all.40.refs_0_, bf16[7,768,768]{2,1,0:T(8,128)(2,1)} %legendre.1.refs_1_, bf16[7,768,768]{2,1,0:T(8,128)(2,1)} %bitcast.34, f32[768,512]{1,0:T(8,128)} %pad.16.refs_3_, f32[768,512]{1,0:T(8,128)} %pad.17.refs_4_, ...), custom_call_target="tpu_custom_call" | custom-call | flops 6442450944 | bytes 18874368 | tf_op jit(solution)/shard_map/middle/pallas_call | solution.py:206
  249.9 9.7 %middle.3 = (bf16[7,720,512]{2,1,0:T(8,128)(2,1)}, bf16[32,4,3,3,8,128]{5,4,3,2,1,0:T(8,128)(2,1)}) custom-call(bf16[128,3,3,8,128]{4,3,2,1,0:T(8,128)(2,1)} %copy-done.2, bf16[7,768,768]{2,1,0:T(8,128)(2,1)} %legendre.1.refs_1_, bf16[7,768,768]{2,1,0:T(8,128)(2,1)} %bitcast.35, f32[768,512]{1,0:T(8,128)} %pad.16.refs_3_, ...), custom_call_target="tpu_custom_call", output_to_operand_aliasing={{0}: (6, {})} | custom-call | flops 4831838208 | bytes 14155776 | tf_op jit(solution)/shard_map/middle/pallas_call | solution.py:206
  259.6 42.0 %all_to_all.41.refs_1_ = bf16[128,3,3,8,128]{4,3,2,1,0:T(8,128)(2,1)} all-to-all(bf16[128,3,3,8,128]{4,3,2,1,0:T(8,128)(2,1)} %bitcast.46), channel_id=1, replica_groups=mesh['lat'=8,'lon'=16] {'lat','lon'}, dimensions={0} | all-to-all | bytes 4718592 | tf_op jit(solution)/shard_map/all_to_all | solution.py:458
  301.6 5.1 %all-to-all-start.3 = ((bf16[128,4,3,8,128]{4,3,2,1,0:T(8,128)(2,1)}), bf16[128,4,3,8,128]{4,3,2,1,0:T(8,128)(2,1)S(1)}, u32[]{:S(2)}, u32[]{:S(2)}) async-start(bf16[128,4,3,8,128]{4,3,2,1,0:T(8,128)(2,1)} %bitcast.44), calls=%async_computation.3 | async-start | bytes 6291456 | tf_op jit(solution)/shard_map/all_to_all | solution.py:458
  306.7 8.3 %copy.61 = bf16[1792,1536]{0,1:T(8,128)(2,1)} copy(bf16[1792,1536]{1,0:T(8,128)(2,1)} %bitcast.33) | data formatting | bytes 11010048 | tf_op jit(solution)/shard_map/convert_element_type | solution.py:442
  315.0 5.3 %multiply_bitcast_fusion.refs_2_ = bf16[1536,1792]{1,0:T(8,128)(2,1)} fusion(bf16[1792,1536]{0,1:T(8,128)(2,1)} %copy.61, bf16[1792]{0:T(1024)(128)(2,1)S(1)} %mul.199), kind=kLoop, calls=%fused_computation.10 | loop fusion | flops 2752512 | bytes 11013632 | tf_op jit(solution)/shard_map/transpose | solution.py:484
  320.4 26.3 %all-to-all-done.3.refs_0_ = bf16[128,4,3,8,128]{4,3,2,1,0:T(8,128)(2,1)S(1)} async-done(((bf16[128,4,3,8,128]{4,3,2,1,0:T(8,128)(2,1)}), bf16[128,4,3,8,128]{4,3,2,1,0:T(8,128)(2,1)S(1)}, u32[]{:S(2)}, u32[]{:S(2)}) %all-to-all-start.3) | async-done | bytes 3145760 | tf_op jit(solution)/shard_map/all_to_all | solution.py:458
  348.4 14.2 %inverse.3 = bf16[16,8,96,128]{3,2,1,0:T(8,128)(2,1)} custom-call(bf16[128,4,3,8,128]{4,3,2,1,0:T(8,128)(2,1)} %copy-done, bf16[128,3,3,8,128]{4,3,2,1,0:T(8,128)(2,1)} %all_to_all.41.refs_1_, bf16[1536,1792]{1,0:T(8,128)(2,1)} %multiply_bitcast_fusion.refs_2_), custom_call_target="tpu_custom_call" | custom-call | flops 5637144576 | bytes 11010048 | tf_op jit(solution)/shard_map/inverse/pallas_call | solution.py:279
  366.5 9.3 %inverse.2 = bf16[16,4,96,128]{3,2,1,0:T(8,128)(2,1)} custom-call(bf16[128,4,3,8,128]{4,3,2,1,0:T(8,128)(2,1)} %copy-done, bf16[128,3,3,8,128]{4,3,2,1,0:T(8,128)(2,1)} %all_to_all.41.refs_1_, bf16[1536,1792]{1,0:T(8,128)(2,1)} %multiply_bitcast_fusion.refs_2_), custom_call_target="tpu_custom_call" | custom-call | flops 2818572288 | bytes 11010048 | tf_op jit(solution)/shard_map/inverse/pallas_call | solution.py:279
  375.9 38.3 %all-to-all-done.7 = bf16[16,8,96,128]{3,2,1,0:T(8,128)(2,1)S(1)} async-done(((bf16[16,8,96,128]{3,2,1,0:T(8,128)(2,1)}), bf16[16,8,96,128]{3,2,1,0:T(8,128)(2,1)S(1)}, u32[]{:S(2)}, u32[]{:S(2)}) %all-to-all-start.7) | async-done | bytes 3145760 | tf_op jit(solution)/shard_map/all_to_all | solution.py:458
  414.2 4.4 all-to-all-start.6
  418.6 11.3 %reshape.304 = bf16[1,7,720,2,256]{4,3,2,1,0:T(2,128)(2,1)} reshape(bf16[7,720,512]{2,1,0:T(8,128)(2,1)} %get-tuple-element.17) | data formatting | bytes 10321920 | tf_op jit(solution)/shard_map/reshape | solution.py:520
  430.0 7.7 %blend.2.refs_2_ = bf16[90,90,256]{2,1,0:T(8,128)(2,1)} custom-call(bf16[4,4,8,96,128]{4,3,2,1,0:T(8,128)(2,1)} %bitcast.37, bf16[90,90,256]{2,1,0:T(8,128)(2,1)} %refs_1_.3), custom_call_target="tpu_custom_call" | custom-call | flops 88473600 | bytes 8847360 | tf_op jit(solution)/shard_map/blend/pallas_call | solution.py:324
  (66 shorter events, 58.0 us)
Async XLA Ops:
  7.4 55.6 %all-to-all-start.1 = ((bf16[16,8,96,128]{3,2,1,0:T(8,128)(2,1)}), bf16[16,8,96,128]{3,2,1,0:T(8,128)(2,1)S(1)}, u32[]{:S(2)}, u32[]{:S(2)}) async-start(bf16[16,8,96,128]{3,2,1,0:T(8,128)(2,1)} %bitcast.36), calls=%async_computation.1 | async-start | bytes 6291456 | tf_op jit(solution)/shard_map/all_to_all | solution.py:458
  15.6 4.8 %copy-start.7 = (s32[128]{0:T(128)S(1)}, s32[128]{0:T(128)}, u32[]{:S(2)}) copy-start(s32[128]{0:T(128)} %param.9) | copy-start | bytes 1540
  15.6 5.2 %copy-start.6 = (s32[720]{0:T(1024)S(1)}, s32[720]{0:T(1024)}, u32[]{:S(2)}) copy-start(s32[720]{0:T(1024)} %param.8) | copy-start | bytes 8644
  63.0 1.7 copy-start.4
  64.7 45.7 %all-to-all-start = ((bf16[16,4,96,128]{3,2,1,0:T(8,128)(2,1)}), bf16[16,4,96,128]{3,2,1,0:T(8,128)(2,1)S(1)}, u32[]{:S(2)}, u32[]{:S(2)}) async-start(bf16[16,4,96,128]{3,2,1,0:T(8,128)(2,1)} %bitcast.42), calls=%async_computation | async-start | bytes 3145728 | tf_op jit(solution)/shard_map/all_to_all | solution.py:458
  110.4 1.1 copy-start.3
  171.5 5.8 %copy-start.5 = (bf16[2,256,256]{2,1,0:T(8,128)(2,1)S(1)}, bf16[2,256,256]{2,1,0:T(8,128)(2,1)}, u32[]{:S(2)}) copy-start(bf16[2,256,256]{2,1,0:T(8,128)(2,1)} %param.7) | copy-start | bytes 786436
  171.5 76.9 %all-to-all-start.4 = ((bf16[128,3,3,8,128]{4,3,2,1,0:T(8,128)(2,1)}), bf16[128,3,3,8,128]{4,3,2,1,0:T(8,128)(2,1)S(1)}, u32[]{:S(2)}, u32[]{:S(2)}) async-start(bf16[128,3,3,8,128]{4,3,2,1,0:T(8,128)(2,1)} %get-tuple-element.14), calls=%async_computation.4 | async-start | bytes 4718592 | tf_op jit(solution)/shard_map/all_to_all | solution.py:458
  248.5 1.4 copy-start.2
  301.6 45.1 %all-to-all-start.3 = ((bf16[128,4,3,8,128]{4,3,2,1,0:T(8,128)(2,1)}), bf16[128,4,3,8,128]{4,3,2,1,0:T(8,128)(2,1)S(1)}, u32[]{:S(2)}, u32[]{:S(2)}) async-start(bf16[128,4,3,8,128]{4,3,2,1,0:T(8,128)(2,1)} %bitcast.44), calls=%async_computation.3 | async-start | bytes 6291456 | tf_op jit(solution)/shard_map/all_to_all | solution.py:458
  346.7 1.7 copy-start
  362.6 51.6 %all-to-all-start.7 = ((bf16[16,8,96,128]{3,2,1,0:T(8,128)(2,1)}), bf16[16,8,96,128]{3,2,1,0:T(8,128)(2,1)S(1)}, u32[]{:S(2)}, u32[]{:S(2)}) async-start(bf16[16,8,96,128]{3,2,1,0:T(8,128)(2,1)} %inverse.3), calls=%async_computation.7 | async-start | bytes 6291456 | tf_op jit(solution)/shard_map/all_to_all | solution.py:458
  414.2 15.8 %copy-start.1 = (bf16[16,8,96,128]{3,2,1,0:T(8,128)(2,1)}, bf16[16,8,96,128]{3,2,1,0:T(8,128)(2,1)S(1)}, u32[]{:S(2)}) copy-start(bf16[16,8,96,128]{3,2,1,0:T(8,128)(2,1)S(1)} %all-to-all-done.7) | copy-start | bytes 9437188
  414.2 27.3 %all-to-all-start.6 = ((bf16[16,4,96,128]{3,2,1,0:T(8,128)(2,1)}), bf16[16,4,96,128]{3,2,1,0:T(8,128)(2,1)}, u32[]{:S(2)}, u32[]{:S(2)}) async-start(bf16[16,4,96,128]{3,2,1,0:T(8,128)(2,1)} %inverse.2), calls=%async_computation.6 | async-start | bytes 3145728 | tf_op jit(solution)/shard_map/all_to_all | solution.py:458

commit v2 on v1

v2 whole, which is shorter than its diff:
```python
import functools
import math

import jax
import jax.numpy as jnp
from jax import lax
from jax.experimental import pallas as pl
from jax.experimental.pallas import tpu as pltpu
from jax.sharding import PartitionSpec as P

QUARTERS = 4
UNIT = 8
UNITS = 3
PAIRS = UNIT // 2
LON_PAD = 96
GROUP = 16
HALF = 64
LANES = 128
SLOTS = 7
LEVELS = 768
ROWS = 768
HOME_CHUNKS = ((0, 3),)
SLOT_CHUNKS = ((0, 3), (3, 7))
VMEM = 60
SEND_VMEM = 54
LESS_VMEM = 28
LEVEL_BLOCK = 128
RESCALE = 8


def call(
    kernel, name, flops, moved, operands, in_specs, after=(), aliases=(), vmem=VMEM, **kwargs
):
    known = len(operands)
    extra = list(after) + list(aliases)

    def body(*refs):
        kernel(*refs[:known], *refs[known + len(extra) :])

    return pl.pallas_call(
        body,
        name=name,
        compiler_params=pltpu.CompilerParams(vmem_limit_bytes=vmem * 1024 * 1024),
        cost_estimate=pl.CostEstimate(flops=flops, bytes_accessed=moved, transcendentals=0),
        in_specs=list(in_specs) + [pl.BlockSpec(memory_space=pl.ANY)] * len(extra),
        input_output_aliases={known + len(after) + i: i for i in range(len(aliases))},
        **kwargs,
    )(*operands, *extra)


def low_half():
    return lax.broadcasted_iota(jnp.int32, (1, LANES), 1) < HALF


def swap(value):
    return pltpu.roll(value, HALF, value.ndim - 1)


def join_low(first, second):
    return jnp.where(low_half(), first, swap(second))


def join_high(first, second):
    return jnp.where(low_half(), swap(first), second)


def exchange_rows(outer, inner):
    row = lax.broadcasted_iota(jnp.int32, (outer * inner, outer * inner), 0)
    column = lax.broadcasted_iota(jnp.int32, (outer * inner, outer * inner), 1)
    return (column == (row % inner) * outer + row // inner).astype(jnp.bfloat16)


def pack_kernel(band_rows, fields_ref, out_ref):
    rows, lon_cols = fields_ref.shape[:2]
    base = pl.program_id(0) * rows
    out_ref[0, :, :, lon_cols:, :] = jnp.zeros(
        (QUARTERS, rows // 2, LON_PAD - lon_cols, LANES), jnp.bfloat16
    )

    def one_pair(pair, carry):
        first = fields_ref[2 * pair].astype(jnp.float32)
        second = fields_ref[2 * pair + 1].astype(jnp.float32)
        first = jnp.where(base + 2 * pair < band_rows, first, 0.0)
        second = jnp.where(base + 2 * pair + 1 < band_rows, second, 0.0)
        for tile in range(2):
            lanes = slice(tile * LANES, (tile + 1) * LANES)
            one, two = first[:, lanes], second[:, lanes]
            out_ref[0, 2 * tile, pair, :lon_cols] = join_low(one, two).astype(jnp.bfloat16)
            out_ref[0, 2 * tile + 1, pair, :lon_cols] = join_high(one, two).astype(jnp.bfloat16)
        return carry

    lax.fori_loop(0, rows // 2, one_pair, 0)


def pack(fields, after):
    band_rows, lon_cols, channels = fields.shape
    rows = UNITS * UNIT
    out = call(
        functools.partial(pack_kernel, band_rows),
        "pack",
        0,
        4 * rows * QUARTERS * LON_PAD * channels,
        operands=[fields],
        after=after,
        vmem=SEND_VMEM,
        grid=(QUARTERS,),
        in_specs=[pl.BlockSpec((rows, lon_cols, channels), lambda q: (q, 0, 0))],
        out_specs=pl.BlockSpec(
            (1, QUARTERS, rows // 2, LON_PAD, LANES), lambda q: (q, 0, 0, 0, 0)
        ),
        out_shape=jax.ShapeDtypeStruct(
            (QUARTERS, QUARTERS, rows // 2, LON_PAD, LANES), jnp.bfloat16
        ),
    )
    return out.reshape(QUARTERS * QUARTERS, rows // 2, LON_PAD, LANES)


def forward_kernel(arrived_ref, table_ref, weight_ref, out_ref, matrix, summed):
    sources = arrived_ref.shape[0]
    slots, _, owners, longitudes = table_ref.shape
    for pair in range(PAIRS):
        matrix[:, pair * LANES : (pair + 1) * LANES] = arrived_ref[:, pair].reshape(
            sources * LON_PAD, LANES
        )
    table = table_ref[...].reshape(slots * 2 * owners, longitudes)
    summed[...] = jnp.dot(table, matrix[...], preferred_element_type=jnp.float32)
    turn = exchange_rows(GROUP, UNIT)
    weights = weight_ref[0]

    def one_slot(slot, carry):
        rows = []
        base = pl.multiple_of(slot * 2 * owners, 2 * owners)
        for pair in range(PAIRS):
            lanes = slice(pair * LANES, (pair + 1) * LANES)
            real = summed[pl.ds(base, owners), lanes] * weights[:, lanes]
            imag = summed[pl.ds(base + owners, owners), lanes] * weights[:, lanes]
            rows.append(join_low(real, imag).astype(jnp.bfloat16))
            rows.append(join_high(real, imag).astype(jnp.bfloat16))
        for first in range(0, owners, 2 * GROUP):
            both = jnp.concatenate(
                [
                    jnp.concatenate([row[start : start + GROUP] for row in rows], axis=0)
                    for start in (first, first + GROUP)
                ],
                axis=1,
            )
            both = jnp.dot(turn, both, preferred_element_type=jnp.float32)
            for half in range(2):
                piece = both[:, half * LANES : (half + 1) * LANES].reshape(GROUP, UNIT, LANES)
                start = first + half * GROUP
                out_ref[start : start + GROUP, slot, 0] = piece.astype(jnp.bfloat16)
        return carry

    lax.fori_loop(0, slots, one_slot, 0)


def forward(arrived, table, weights, slots, after=()):
    start, stop = slots
    sources = arrived.shape[0]
    owners, longitudes = table.shape[2:]
    work = UNITS * (stop - start)
    return call(
        forward_kernel,
        "forward",
        2 * work * 2 * owners * longitudes * PAIRS * LANES,
        2 * (arrived.size + (stop - start) * 2 * owners * longitudes),
        operands=[arrived, table, weights],
        after=after,
        vmem=SEND_VMEM,
        grid=(UNITS,),
        in_specs=[
            pl.BlockSpec((sources, PAIRS, LON_PAD, LANES), lambda u: (0, u, 0, 0)),
            pl.BlockSpec((stop - start, 2, owners, longitudes), lambda u: (0, 0, 0, 0)),
            pl.BlockSpec((1, 1, PAIRS * LANES), lambda u: (u, 0, 0)),
        ],
        out_specs=pl.BlockSpec(
            (owners, stop - start, 1, UNIT, LANES), lambda u: (0, 0, u, 0, 0)
        ),
        out_shape=jax.ShapeDtypeStruct((owners, stop - start, UNITS, UNIT, LANES), jnp.bfloat16),
        scratch_shapes=[
            pltpu.VMEM((sources * LON_PAD, PAIRS * LANES), jnp.bfloat16),
            pltpu.VMEM(((stop - start) * 2 * owners, PAIRS * LANES), jnp.float32),
        ],
    )


def middle_kernel(arrived_ref, table_ref, gain_ref, mixing_ref, spectrum_ref, out_ref):
    degrees, width = gain_ref.shape
    arrived = arrived_ref[:, 0].astype(jnp.float32)
    groups = arrived.shape[0] // QUARTERS
    arrived = arrived.reshape(groups, QUARTERS, UNITS * UNIT, LANES)
    columns = jnp.concatenate(
        [
            arrived[:, quarter].reshape(ROWS, LANES).astype(jnp.bfloat16)
            for quarter in range(QUARTERS)
        ],
        axis=1,
    )
    spectra = jnp.dot(table_ref[0, :degrees], columns, preferred_element_type=jnp.float32)
    parts = []
    for quarter in range(QUARTERS):
        tile = quarter // 2
        real = gain_ref[:, tile * LANES : (tile + 1) * LANES]
        imag = gain_ref[:, (2 + tile) * LANES : (3 + tile) * LANES]
        join = join_high if quarter % 2 else join_low
        piece = spectra[:, quarter * LANES : (quarter + 1) * LANES]
        piece = join(real, real) * piece + join(-imag, imag) * swap(piece)
        parts.append(piece.astype(jnp.bfloat16))
    scaled = jnp.concatenate(parts, axis=1)
    mixed = jnp.dot(scaled, mixing_ref[...], preferred_element_type=jnp.float32)
    pieces = [mixed[:, q * LANES : (q + 1) * LANES] for q in range(QUARTERS)]
    for tile in range(2):
        one, two = pieces[2 * tile], pieces[2 * tile + 1]
        lanes = slice(tile * LANES, (tile + 1) * LANES)
        spectrum_ref[0, :, lanes] = join_low(one, two).astype(jnp.bfloat16)
        lanes = slice((2 + tile) * LANES, (3 + tile) * LANES)
        spectrum_ref[0, :, lanes] = join_high(one, two).astype(jnp.bfloat16)
    filled = jnp.concatenate(
        [mixed.astype(jnp.bfloat16), jnp.zeros((LEVELS - degrees, width), jnp.bfloat16)], axis=0
    )
    returned = lax.dot_general(
        table_ref[0], filled, (((0,), (0,)), ((), ())), preferred_element_type=jnp.float32
    )
    for quarter in range(QUARTERS):
        piece = returned[:, quarter * LANES : (quarter + 1) * LANES]
        out_ref[:, quarter, 0] = piece.reshape(groups, UNITS, UNIT, LANES).astype(jnp.bfloat16)


def middle(arrived, table, gain, mixing, slots, after=()):
    start, stop = slots
    owners = arrived.shape[0]
    groups = owners // QUARTERS
    degrees, width = gain.shape
    spectrum, out = call(
        middle_kernel,
        "middle",
        2 * (stop - start) * LEVELS * width * (2 * ROWS + width),
        (stop - start) * (4 * LEVELS * ROWS + 6 * LEVELS * width),
        operands=[arrived, table, gain, mixing],
        after=after,
        grid=(stop - start,),
        in_specs=[
            pl.BlockSpec((owners, 1, UNITS, UNIT, LANES), lambda s: (0, s, 0, 0, 0)),
            pl.BlockSpec((1, LEVELS, ROWS), lambda s: (start + s, 0, 0)),
            pl.BlockSpec(gain.shape, lambda s: (0, 0)),
            pl.BlockSpec(mixing.shape, lambda s: (0, 0)),
        ],
        out_specs=[
            pl.BlockSpec((1, degrees, width), lambda s: (s, 0, 0)),
            pl.BlockSpec((groups, QUARTERS, 1, UNITS, UNIT, LANES), lambda s: (0, 0, s, 0, 0, 0)),
        ],
        out_shape=[
            jax.ShapeDtypeStruct((stop - start, degrees, width), jnp.bfloat16),
            jax.ShapeDtypeStruct(
                (groups, QUARTERS, stop - start, UNITS, UNIT, LANES), jnp.bfloat16
            ),
        ],
    )
    return spectrum, out.reshape(owners, stop - start, UNITS, UNIT, LANES)


def inverse_kernel(scale, has_partial, *refs):
    arrived_ref, table_ref = refs[:2]
    partial_ref = refs[2] if has_partial else None
    out_ref, matrix = refs[-2:]
    owners, slots = arrived_ref.shape[:2]

    def one_slot(slot, carry):
        row = pl.multiple_of(slot * 2 * owners, 2 * owners)
        turn = exchange_rows(UNIT, GROUP)
        wide = arrived_ref[:, slot, 0].astype(jnp.float32).reshape(owners * UNIT, LANES)
        wide = wide.astype(jnp.bfloat16)
        size = GROUP * UNIT
        groups = []
        for first in range(0, owners * UNIT, 2 * size):
            both = jnp.concatenate(
                [wide[first : first + size], wide[first + size : first + 2 * size]], axis=1
            )
            both = jnp.dot(turn, both, preferred_element_type=jnp.float32)
            groups += [both[:, :LANES], both[:, LANES:]]
        for pair in range(PAIRS):
            one, two = [
                jnp.concatenate([g[k * GROUP : (k + 1) * GROUP] for g in groups], axis=0)
                for k in (2 * pair, 2 * pair + 1)
            ]
            lanes = slice(pair * LANES, (pair + 1) * LANES)
            matrix[pl.ds(row, owners), lanes] = join_low(one, two).astype(jnp.bfloat16)
            matrix[pl.ds(row + owners, owners), lanes] = join_high(one, two).astype(
                jnp.bfloat16
            )
        return carry

    lax.fori_loop(0, slots, one_slot, 0)

    summed = jnp.dot(table_ref[...], matrix[...], preferred_element_type=jnp.float32)
    if not has_partial:
        out_ref[0] = summed
        return
    summed = ((summed + partial_ref[0]) * scale).astype(jnp.bfloat16)
    for pair in range(PAIRS):
        lanes = slice(pair * LANES, (pair + 1) * LANES)
        out_ref[:, pair] = summed[:, lanes].reshape(-1, LON_PAD, LANES)


def inverse(arrived, table, chunk, lon_total, partial=None, after=()):
    first, last = chunk
    count = last - first
    owners, slots = arrived.shape[:2]
    targets = table.shape[0] // LON_PAD
    has_partial = partial is not None
    summed = pl.BlockSpec((1, table.shape[0], PAIRS * LANES), lambda u: (u, 0, 0))
    if has_partial:
        spec = pl.BlockSpec((targets, PAIRS, LON_PAD, LANES), lambda u: (0, u, 0, 0))
        shape = jax.ShapeDtypeStruct((targets, count * PAIRS, LON_PAD, LANES), jnp.bfloat16)
    else:
        spec = summed
        shape = jax.ShapeDtypeStruct((count, table.shape[0], PAIRS * LANES), jnp.float32)
    return call(
        functools.partial(inverse_kernel, 1.0 / lon_total, has_partial),
        "inverse",
        2 * count * table.size * PAIRS * LANES,
        2 * 2 * table.size,
        operands=[arrived, table] + ([partial] if has_partial else []),
        after=after,
        vmem=SEND_VMEM if has_partial else VMEM,
        grid=(count,),
        in_specs=[
            pl.BlockSpec((owners, slots, 1, UNIT, LANES), lambda u: (0, 0, first + u, 0, 0)),
            pl.BlockSpec(table.shape, lambda u: (0, 0)),
        ]
        + ([summed] if has_partial else []),
        out_specs=spec,
        out_shape=shape,
        scratch_shapes=[pltpu.VMEM((table.shape[1], PAIRS * LANES), jnp.bfloat16)],
    )


def blend_kernel(arrived_ref, fields_ref, out_ref):
    lon_cols = fields_ref.shape[1]

    def gelu(value):
        return 0.5 * value * (1.0 + lax.erf(value * math.sqrt(0.5)))

    for pair in range(PAIRS):
        for tile in range(2):
            lanes = slice(tile * LANES, (tile + 1) * LANES)
            one = gelu(arrived_ref[0, 2 * tile, pair, :lon_cols].astype(jnp.float32))
            two = gelu(arrived_ref[0, 2 * tile + 1, pair, :lon_cols].astype(jnp.float32))
            for row, value in ((2 * pair, join_low(one, two)), (2 * pair + 1, join_high(one, two))):
                held = fields_ref[row, :, lanes].astype(jnp.float32)
                out_ref[row, :, lanes] = (held + value).astype(jnp.bfloat16)


def blend(arrived, fields, chunk, buffer):
    first, last = chunk
    count = last - first
    band_rows, lon_cols, channels = fields.shape
    arrived = arrived.reshape(QUARTERS, QUARTERS, count * PAIRS, LON_PAD, LANES)
    held = pl.BlockSpec((UNIT, lon_cols, channels), lambda q, u: (q * UNITS + first + u, 0, 0))
    return call(
        blend_kernel,
        "blend",
        60 * count * UNIT * QUARTERS * lon_cols * channels,
        6 * count * UNIT * QUARTERS * lon_cols * channels,
        operands=[arrived, fields],
        vmem=LESS_VMEM,
        aliases=[] if buffer is None else [buffer],
        grid=(QUARTERS, count),
        in_specs=[
            pl.BlockSpec(
                (1, QUARTERS, PAIRS, LON_PAD, LANES),
                lambda q, u: (q, 0, u, 0, 0),
            ),
            pl.BlockSpec(held.block_shape, held.index_map),
        ],
        out_specs=held,
        out_shape=jax.ShapeDtypeStruct(fields.shape, fields.dtype),
    )


def legendre_kernel(degrees, order_ref, start_ref, lat_ref, out_ref, state, rows):
    tiles = ROWS // LANES
    order = order_ref[...]

    @pl.when(pl.program_id(0) == 0)
    def _():
        for tile in range(tiles):
            lanes = slice(tile * LANES, (tile + 1) * LANES)
            state[0, :, lanes] = jnp.zeros_like(order)
            state[1, :, lanes] = jnp.ones_like(order)
            state[2, :, lanes] = start_ref[...] + order * jnp.log(lat_ref[1:2, lanes])

    def pieces(index):
        return tuple(state[index, :, t * LANES : (t + 1) * LANES] for t in range(tiles))

    cosines = tuple(lat_ref[0:1, t * LANES : (t + 1) * LANES] for t in range(tiles))
    first = pl.program_id(0) * LEVEL_BLOCK

    def group(index, carry):
        previous, current, log_scale = [list(part) for part in carry]
        halves = []
        for tile in range(tiles):
            largest = jnp.maximum(jnp.abs(previous[tile]), jnp.abs(current[tile]))
            shrink = 1.0 / largest
            previous[tile] = previous[tile] * shrink
            current[tile] = current[tile] * shrink
            log_scale[tile] = log_scale[tile] + jnp.log(largest)
            halves.append(jnp.exp(0.5 * log_scale[tile]))
        for inner in range(RESCALE):
            level = (first + index * RESCALE + inner).astype(jnp.float32)
            square = (level - 1.0) * (level - 1.0)
            upper = jnp.sqrt(
                jnp.maximum(4.0 * level * level - 1.0, 0.0)
                / jnp.maximum(level * level - order * order, 1.0)
            )
            lower = jnp.sqrt(
                jnp.maximum(square - order * order, 0.0) / jnp.maximum(4.0 * square - 1.0, 1.0)
            )
            moving = level > order
            shown = jnp.logical_and(level >= order, level < degrees)
            row = pl.multiple_of((index * RESCALE + inner) * 8, 8)
            for tile in range(tiles):
                advanced = upper * (cosines[tile] * current[tile] - lower * previous[tile])
                previous[tile] = jnp.where(moving, current[tile], previous[tile])
                current[tile] = jnp.where(moving, advanced, current[tile])
                value = (current[tile] * halves[tile]) * halves[tile]
                rows[tile, pl.ds(row, 8), :] = jnp.where(shown, value, 0.0)
        return tuple(previous), tuple(current), tuple(log_scale)

    done = lax.fori_loop(
        0, LEVEL_BLOCK // RESCALE, group, (pieces(0), pieces(1), pieces(2))
    )
    for index in range(3):
        for tile in range(tiles):
            state[index, :, tile * LANES : (tile + 1) * LANES] = done[index][tile]
    for slot in range(SLOTS):
        for tile in range(tiles):
            out_ref[slot, :, tile * LANES : (tile + 1) * LANES] = rows[
                tile, pl.ds(slot, LEVEL_BLOCK, stride=8), :
            ].astype(jnp.bfloat16)


def legendre(orders, colatitude, degrees, after):
    order_col = orders.astype(jnp.float32)
    half_gamma = 0.5 * math.log(math.pi) - math.log(2.0)
    log_start = -0.5 * math.log(2.0) + 0.5 * (
        lax.lgamma(order_col + 1.5) - half_gamma - lax.lgamma(order_col + 1.0)
    )
    widen = lambda a: jnp.broadcast_to(jnp.pad(a, (0, 8 - SLOTS))[:, None], (8, LANES))
    lat = jnp.stack([jnp.cos(colatitude), jnp.sin(colatitude)])
    return call(
        functools.partial(legendre_kernel, degrees),
        "legendre",
        30 * LEVELS * 8 * ROWS,
        2 * SLOTS * LEVELS * ROWS,
        operands=[widen(order_col), widen(log_start), lat],
        after=after,
        grid=(LEVELS // LEVEL_BLOCK,),
        in_specs=[
            pl.BlockSpec((8, LANES), lambda i: (0, 0)),
            pl.BlockSpec((8, LANES), lambda i: (0, 0)),
            pl.BlockSpec((2, ROWS), lambda i: (0, 0)),
        ],
        out_specs=pl.BlockSpec((SLOTS, LEVEL_BLOCK, ROWS), lambda i: (0, i, 0)),
        out_shape=jax.ShapeDtypeStruct((SLOTS, LEVELS, ROWS), jnp.bfloat16),
        scratch_shapes=[
            pltpu.VMEM((3, 8, ROWS), jnp.float32),
            pltpu.VMEM((ROWS // LANES, LEVEL_BLOCK * 8, LANES), jnp.float32),
        ],
    )


def sine_turn(turn):
    angle = turn * (2.0 * math.pi)
    square = angle * angle
    total = jnp.full_like(angle, -1.0 / math.factorial(11))
    for power, sign in ((9, 1.0), (7, -1.0), (5, 1.0), (3, -1.0), (1, 1.0)):
        total = total * square + sign / math.factorial(power)
    return total * angle


def fourier_kernel(lon_total, first_slot, list_ref, count_ref, longitude_ref, out_ref):
    owners = count_ref.shape[1]
    modes = list_ref.shape[1]
    tiles = longitude_ref.shape[1] // LANES
    slot = first_slot + pl.program_id(0)
    row = lax.broadcasted_iota(jnp.int32, (owners, owners), 0)
    column = lax.broadcasted_iota(jnp.int32, (owners, owners), 1)
    counts = count_ref[...]
    start = jnp.sum(jnp.where(column < row, counts, 0.0), axis=1, keepdims=True)
    count = jnp.sum(jnp.where(column == row, counts, 0.0), axis=1, keepdims=True)
    mode = lax.broadcasted_iota(jnp.int32, (owners, modes), 1).astype(jnp.float32)
    found = mode == start + slot.astype(jnp.float32)
    order = jnp.sum(jnp.where(found, list_ref[...], 0.0), axis=1, keepdims=True)
    order = jnp.where(slot.astype(jnp.float32) < count, order, -1.0)
    order = jnp.broadcast_to(order, (owners, LANES))
    rest = order - 4.0 * jnp.floor(order * 0.25)
    quarter_cosine = jnp.where(rest == 0.0, 1.0, 0.0) - jnp.where(rest == 2.0, 1.0, 0.0)
    quarter_sine = jnp.where(rest == 1.0, 1.0, 0.0) - jnp.where(rest == 3.0, 1.0, 0.0)
    for tile in range(tiles // 4):
        longitude = longitude_ref[:, tile * LANES : (tile + 1) * LANES]
        product = order * longitude
        wrapped = product - lon_total * jnp.floor(product * (1.0 / lon_total) + 0.5)
        turn = wrapped * (1.0 / lon_total)
        size = jnp.abs(turn)
        cosine = sine_turn(0.25 - jnp.minimum(size, 0.5))
        folded = jnp.where(size > 0.25, jnp.where(turn < 0, -0.5, 0.5) - turn, turn)
        live = jnp.logical_and(order >= 0.0, longitude >= 0.0)
        cosine = jnp.where(live, cosine, 0.0)
        sine = jnp.where(live, -sine_turn(folded), 0.0)
        for quarter in range(4):
            place = quarter * (tiles // 4) + tile
            lanes = slice(place * LANES, (place + 1) * LANES)
            out_ref[0, 0, :, lanes] = cosine.astype(jnp.bfloat16)
            out_ref[0, 1, :, lanes] = sine.astype(jnp.bfloat16)
            cosine, sine = (
                quarter_cosine * cosine + quarter_sine * sine,
                quarter_cosine * sine - quarter_sine * cosine,
            )


def fourier_table(column_list, column_counts, slots, lon_devices, lon_cols, after=()):
    start, stop = slots
    owners = column_counts.shape[0]
    modes = -(-column_list.shape[0] // LANES) * LANES
    place = jnp.arange(lon_devices * LON_PAD, dtype=jnp.int32)
    block, inside = place // LON_PAD, place % LON_PAD
    longitude = jnp.where(inside < lon_cols, block * lon_cols + inside, -1)
    shape = (stop - start, 2, owners, place.size)
    return call(
        functools.partial(fourier_kernel, lon_devices * lon_cols, start),
        "fourier",
        20 * math.prod(shape),
        2 * math.prod(shape),
        operands=[
            jnp.pad(column_list, (0, modes - column_list.shape[0])).astype(jnp.float32)[None, :],
            column_counts.astype(jnp.float32)[None, :],
            longitude.astype(jnp.float32)[None, :],
        ],
        after=after,
        grid=(stop - start,),
        in_specs=[
            pl.BlockSpec((1, modes), lambda s: (0, 0)),
            pl.BlockSpec((1, owners), lambda s: (0, 0)),
            pl.BlockSpec((1, place.size), lambda s: (0, 0)),
        ],
        out_specs=pl.BlockSpec((1, *shape[1:]), lambda s: (s, 0, 0, 0)),
        out_shape=jax.ShapeDtypeStruct(shape, jnp.bfloat16),
    )


def regroup(array, axis):
    shape = array.shape
    split = shape[:axis] + (2, QUARTERS, HALF) + shape[axis + 1 :]
    return jnp.swapaxes(array.reshape(split), axis, axis + 1).reshape(shape)


def complex_block(mix_weight):
    top_half = jnp.concatenate([mix_weight[0], mix_weight[1]], axis=1)
    bottom_half = jnp.concatenate([-mix_weight[1], mix_weight[0]], axis=1)
    return jnp.concatenate([top_half, bottom_half], axis=0)


def exchange(array, axes):
    flat = array.reshape(array.shape[0], -1, LANES)
    flat = lax.all_to_all(flat, axes, split_axis=0, concat_axis=0, tiled=True)
    return flat.reshape(array.shape)


def shards(fields, spectral_gain, mix_weight, column_list, column_counts):
    band_rows, lon_cols, channels = fields.shape
    lat_devices = lax.axis_size("lat")
    lon_devices = lax.axis_size("lon")
    owners = lat_devices * lon_devices
    lat_total = band_rows * lat_devices
    lon_total = lon_cols * lon_devices
    degrees = spectral_gain.shape[0]
    mode_count = column_list.shape[0]

    run_ends = jnp.cumsum(column_counts)
    starts = run_ends - column_counts
    offsets = jnp.arange(SLOTS, dtype=jnp.int32)
    positions = jnp.minimum(starts[None, :] + offsets[:, None], mode_count - 1)
    matches = positions[:, :, None] == jnp.arange(mode_count, dtype=jnp.int32)
    slot_orders = jnp.sum(jnp.where(matches, column_list, 0), axis=2)
    owner_index = lax.axis_index(("lat", "lon"))
    own_orders = lax.dynamic_slice_in_dim(slot_orders, owner_index, 1, axis=1)[:, 0]
    padded = jnp.arange(ROWS, dtype=jnp.int32)
    band, inside = padded // (ROWS // lat_devices), padded % (ROWS // lat_devices)
    row = (band * band_rows + jnp.minimum(inside, band_rows - 1)).astype(jnp.float32)
    colatitude = math.pi * (row + 0.5) / lat_total

    group = lax.axis_index("lon") // QUARTERS
    mine = jnp.arange(UNITS * UNIT, dtype=jnp.int32) + group * (UNITS * UNIT)
    mine = (lax.axis_index("lat") * band_rows + mine).astype(jnp.float32)
    weights = math.pi / lat_total * jnp.sin(math.pi * (mine + 0.5) / lat_total)
    weights = jnp.repeat(weights.reshape(UNITS, 1, UNIT), HALF, axis=2)
    gain = spectral_gain.reshape(degrees, 2 * channels)
    mixing = regroup(regroup(complex_block(mix_weight), 0), 1)

    def fourier(slots, after=()):
        return fourier_table(column_list, column_counts, slots, lon_devices, lon_cols, after)

    def turned(table, slots):
        factor = jnp.where(slot_orders[slice(*slots)] == 0, 1.0, 2.0).astype(jnp.bfloat16)
        return (table * factor[:, None, :, None]).reshape(-1, lon_devices * LON_PAD).T

    early, late = SLOT_CHUNKS
    early_table = fourier(early)
    gathered = exchange(pack(fields, (early_table, weights)), "lon")
    send = forward(gathered, early_table, weights, early)
    early_arrived = exchange(send, ("lat", "lon"))
    late_table = fourier(late, (send,))
    send = forward(gathered, late_table, weights, late)
    late_arrived = exchange(send, ("lat", "lon"))
    associated = legendre(own_orders, colatitude, degrees, (send,))
    early_spectrum, send = middle(early_arrived, associated, gain, mixing, early)
    early_landed = exchange(send, ("lat", "lon"))
    early_back, late_back = turned(early_table, early), turned(late_table, late)
    late_spectrum, send = middle(
        late_arrived, associated, gain, mixing, late, (early_back, late_back)
    )
    late_landed = exchange(send, ("lat", "lon"))
    spectrum = jnp.concatenate([early_spectrum, late_spectrum])
    partials = [inverse(early_landed, early_back, chunk, lon_total) for chunk in HOME_CHUNKS]
    spectrum = spectrum.reshape(1, SLOTS, degrees, 2, channels)
    sends = [
        inverse(late_landed, late_back, chunk, lon_total, partial, (spectrum,))
        for chunk, partial in zip(HOME_CHUNKS, partials)
    ]
    homes = [exchange(send, "lon") for send in sends]
    blended = None
    for chunk, home in zip(HOME_CHUNKS, homes):
        blended = blend(home, fields, chunk, blended)
    return blended, spectrum


def solution(mesh):
    placed = (P("lat", "lon", None), P(), P(), P(), P())
    return jax.shard_map(
        shards,
        mesh=mesh,
        in_specs=placed,
        out_specs=(P("lat", "lon", None), P(("lat", "lon"), None, None, None, None)),
        check_vma=False,
    )
```

time: 448 us -> 345 us (0.77)
  waiting for transfers between devices: 110 us -> 44.7 us
  local copies, waits for them, and re-layouts: 68.7 us -> 30.7 us
  blocking collectives: 92.6 us -> 125 us
  other arithmetic: 33.4 us -> 13.2 us
  starting transfers between devices: 31.4 us -> 22.7 us
    all_to_all x6 -> x4, waiting for transfers between devices: 110 us -> 44.7 us  [exchange(): flat = lax.all_to_all(flat, axes, split_axis=0, concat_axis=0, tiled=True)]
    all_to_all x2, blocking collectives: 92.6 us -> 125 us  [exchange(): flat = lax.all_to_all(flat, axes, split_axis=0, concat_axis=0, tiled=True)]
    mul x1 -> x2, other arithmetic: 23.1 us -> 3.57 us  [turned(): table * factor[:, None, :, None]]
    pallas_call x1 -> x0, local copies, waits for them, and re-layouts: 11.8 us -> none  [legendre(): call(functools.partial(legendre_kernel, degrees), 'legendre', 30 * LEVELS...]
    reshape x1 -> x3, local copies, waits for them, and re-layouts: 11.3 us -> 20.4 us  [the longest x1 11.3 us: shards(): spectrum = spectrum.reshape(1, SLOTS, degrees, 2, channels)]
    all_to_all x6 -> x4, starting transfers between devices: 31.4 us -> 22.7 us  [exchange(): flat = lax.all_to_all(flat, axes, split_axis=0, concat_axis=0, tiled=True)]
    convert_element_type x1 -> x0, local copies, waits for them, and re-layouts: 8.33 us -> none  [fourier_tables(): jnp.stack([jnp.cos(angles) * mask, -jnp.sin(angles) * mask], axis=1)]
    reshape x4 -> x2, local copies, waits for them, and re-layouts: 8.83 us -> 1.05 us  [regroup(): return jnp.swapaxes(array.reshape(split), axis, axis + 1).reshape(shape)]
  transfers between devices with their start and end apart: 6 -> 4, of which waited for: 4 -> 4; matrix products, arithmetic and copies ran while one was open for 22% -> 10% of each run, Pallas kernels for 14% -> 19%
where the time goes in v2:
time: 345 us; the launch traced here: 344 us
  blocking collectives  125 us (36%)
  Pallas kernels  106 us (31%)
  waiting for transfers between devices  44.7 us (13%)
  local copies, waits for them, and re-layouts  30.7 us (9%)
  starting transfers between devices  22.7 us (7%)
  other arithmetic  13.2 us (4%)
    all_to_all x2, blocking collectives, exchange(): flat = lax.all_to_all(flat, axes, split_axis=0, concat_axis=0, tiled=True)  125 us
    pallas_call x11, Pallas kernels, call(): pl.pallas_call(body, name=name, compiler_params=pltpu.CompilerParams(vmem...  106 us
    all_to_all x4, waiting for transfers between devices, exchange(): flat = lax.all_to_all(flat, axes, split_axis=0, concat_axis=0, tiled=True)  44.7 us
    all_to_all x4, starting transfers between devices, exchange(): flat = lax.all_to_all(flat, axes, split_axis=0, concat_axis=0, tiled=True)  22.7 us
    reshape x1, local copies, waits for them, and re-layouts, shards(): spectrum = spectrum.reshape(1, SLOTS, degrees, 2, channels)  11.3 us
    reshape x2, local copies, waits for them, and re-layouts, turned(): (table * factor[:, None, :, None]).reshape(-1, lon_devices * LON_PAD)  9.09 us
  transfers between devices with their start and end apart: 4, of which 4 were waited for; matrix products, arithmetic and copies ran while one was open for 10% of the time, Pallas kernels for 19%

profile of v2, /device:TPU:0, one launch (start us, length us, event | category | flops | bytes accessed | tf_op | source)
XLA Modules:
  0.0 343.5 jit_solution(13230796947935485811)
XLA Ops:
  9.5 7.6 %pack.1 = bf16[4,4,12,96,128]{4,3,2,1,0:T(8,128)(2,1)} custom-call(bf16[90,90,256]{2,1,0:T(8,128)(2,1)} %refs_1_.1, bf16[3,2,128,1536]{3,2,1,0:T(8,128)(2,1)} %fourier.2.refs_1_, f32[3,1,512]{2,1,0:T(1,128)} %broadcast_in_dim.63.refs_2_), custom_call_target="tpu_custom_call" | custom-call | bytes 9437184 | tf_op jit(solution)/shard_map/pack/pallas_call | solution.py:40
  17.1 64.7 %all_to_all.30 = bf16[16,1152,128]{2,1,0:T(8,128)(2,1)} all-to-all(bf16[16,1152,128]{2,1,0:T(8,128)(2,1)} %bitcast.38), channel_id=1, replica_groups=mesh['lat'=8,'lon'=16] {'lon'}, dimensions={0} | all-to-all | bytes 9437184 | tf_op jit(solution)/shard_map/all_to_all | solution.py:566
  81.8 10.5 %forward.2.refs_3_ = bf16[128,3,3,8,128]{4,3,2,1,0:T(8,128)(2,1)} custom-call(bf16[16,12,96,128]{3,2,1,0:T(8,128)(2,1)} %bitcast.49, bf16[3,2,128,1536]{3,2,1,0:T(8,128)(2,1)} %fourier.2.refs_1_, f32[3,1,512]{2,1,0:T(1,128)} %broadcast_in_dim.63.refs_2_), custom_call_target="tpu_custom_call" | custom-call | flops 3623878656 | bytes 7077888 | tf_op jit(solution)/shard_map/forward/pallas_call | solution.py:40
  92.3 6.2 %all-to-all-start.3 = ((bf16[128,72,128]{2,1,0:T(8,128)(2,1)}), bf16[128,72,128]{2,1,0:T(8,128)(2,1)S(1)}, u32[]{:S(2)}, u32[]{:S(2)}) async-start(bf16[128,72,128]{2,1,0:T(8,128)(2,1)} %bitcast.48), calls=%async_computation.3 | async-start | bytes 4718592 | tf_op jit(solution)/shard_map/all_to_all | solution.py:566
  98.5 4.5 %fourier.3.refs_1_ = bf16[4,2,128,1536]{3,2,1,0:T(8,128)(2,1)} custom-call(f32[1,768]{1,0:T(1,128)} %broadcast_in_dim.60.refs_0_, f32[1,128]{1,0:T(1,128)} %get-tuple-element.13.refs_1_, f32[1,1536]{1,0:T(1,128)} %fusion.2.refs_2_, bf16[128,3,3,8,128]{4,3,2,1,0:T(8,128)(2,1)} %forward.2.refs_3_), custom_call_target="tpu_custom_call" | custom-call | flops 31457280 | bytes 3145728 | tf_op jit(solution)/shard_map/fourier/pallas_call | solution.py:40
  103.0 13.2 %forward.3.refs_3_ = bf16[128,4,3,8,128]{4,3,2,1,0:T(8,128)(2,1)} custom-call(bf16[16,12,96,128]{3,2,1,0:T(8,128)(2,1)} %bitcast.50, bf16[4,2,128,1536]{3,2,1,0:T(8,128)(2,1)} %fourier.3.refs_1_, f32[3,1,512]{2,1,0:T(1,128)} %broadcast_in_dim.63.refs_2_), custom_call_target="tpu_custom_call" | custom-call | flops 4831838208 | bytes 7864320 | tf_op jit(solution)/shard_map/forward/pallas_call | solution.py:40
  116.2 14.7 %all-to-all-done.3 = bf16[128,72,128]{2,1,0:T(8,128)(2,1)S(1)} async-done(((bf16[128,72,128]{2,1,0:T(8,128)(2,1)}), bf16[128,72,128]{2,1,0:T(8,128)(2,1)S(1)}, u32[]{:S(2)}, u32[]{:S(2)}) %all-to-all-start.3) | async-done | bytes 2359328 | tf_op jit(solution)/shard_map/all_to_all | solution.py:566
  132.3 5.7 %all-to-all-start.1 = ((bf16[128,96,128]{2,1,0:T(8,128)(2,1)}), bf16[128,96,128]{2,1,0:T(8,128)(2,1)}, u32[]{:S(2)}, u32[]{:S(2)}) async-start(bf16[128,96,128]{2,1,0:T(8,128)(2,1)} %bitcast.40), calls=%async_computation.1 | async-start | bytes 6291456 | tf_op jit(solution)/shard_map/all_to_all | solution.py:566
  144.6 16.1 %legendre.1.refs_1_ = bf16[7,768,768]{2,1,0:T(8,128)(2,1)} custom-call(f32[8,128]{1,0:T(8,128)} %broadcast_in_dim.66.refs_0_, f32[8,128]{1,0:T(8,128)} %broadcast_in_dim.67.refs_1_, f32[2,768]{1,0:T(2,128)} %pad_maximum_fusion.1.refs_2_, bf16[128,4,3,8,128]{4,3,2,1,0:T(8,128)(2,1)} %forward.3.refs_3_), custom_call_target="tpu_custom_call" | custom-call | flops 141557760 | bytes 8257536 | tf_op jit(solution)/shard_map/legendre/pallas_call | solution.py:40
  160.8 8.7 %middle.3 = (bf16[3,720,512]{2,1,0:T(8,128)(2,1)}, bf16[32,4,3,3,8,128]{5,4,3,2,1,0:T(8,128)(2,1)}) custom-call(bf16[128,3,3,8,128]{4,3,2,1,0:T(8,128)(2,1)} %bitcast.53, bf16[7,768,768]{2,1,0:T(8,128)(2,1)} %legendre.1.refs_1_, f32[720,512]{1,0:T(8,128)} %bitcast.59, bf16[512,512]{1,0:T(8,128)(2,1)} %copy.33.refs_3_), custom_call_target="tpu_custom_call" | custom-call | flops 4831838208 | bytes 14155776 | tf_op jit(solution)/shard_map/middle/pallas_call | solution.py:40
  169.5 8.4 %all-to-all-done.1 = bf16[128,96,128]{2,1,0:T(8,128)(2,1)} async-done(((bf16[128,96,128]{2,1,0:T(8,128)(2,1)}), bf16[128,96,128]{2,1,0:T(8,128)(2,1)}, u32[]{:S(2)}, u32[]{:S(2)}) %all-to-all-start.1) | async-done | bytes 3145760 | tf_op jit(solution)/shard_map/all_to_all | solution.py:566
  177.9 5.9 %all-to-all-start.4 = ((bf16[128,72,128]{2,1,0:T(8,128)(2,1)}), bf16[128,72,128]{2,1,0:T(8,128)(2,1)}, u32[]{:S(2)}, u32[]{:S(2)}) async-start(bf16[128,72,128]{2,1,0:T(8,128)(2,1)} %bitcast.54), calls=%async_computation.4 | async-start | bytes 4718592 | tf_op jit(solution)/shard_map/all_to_all | solution.py:566
  185.5 4.4 %copy.35 = bf16[768,1536]{0,1:T(8,128)(2,1)} copy(bf16[768,1536]{1,0:T(8,128)(2,1)} %bitcast.47) | data formatting | bytes 4718592 | tf_op jit(solution)/shard_map/reshape | solution.py:606
  191.9 4.7 %copy.36 = bf16[1024,1536]{0,1:T(8,128)(2,1)} copy(bf16[1024,1536]{1,0:T(8,128)(2,1)} %bitcast.41) | data formatting | bytes 6291456 | tf_op jit(solution)/shard_map/reshape | solution.py:606
  196.5 10.6 %middle.2 = (bf16[4,720,512]{2,1,0:T(8,128)(2,1)}, bf16[32,4,4,3,8,128]{5,4,3,2,1,0:T(8,128)(2,1)}) custom-call(bf16[128,4,3,8,128]{4,3,2,1,0:T(8,128)(2,1)} %bitcast.4.refs_0_, bf16[7,768,768]{2,1,0:T(8,128)(2,1)} %legendre.1.refs_1_, f32[720,512]{1,0:T(8,128)} %bitcast.60, bf16[512,512]{1,0:T(8,128)(2,1)} %copy.33.refs_3_, bf16[1536,768]{1,0:T(8,128)(2,1)} %bitcast.45, ...), custom_call_target="tpu_custom_call" | custom-call | flops 6442450944 | bytes 18874368 | tf_op jit(solution)/shard_map/middle/pallas_call | solution.py:40
  207.1 8.5 %all-to-all-done.4 = bf16[128,72,128]{2,1,0:T(8,128)(2,1)} async-done(((bf16[128,72,128]{2,1,0:T(8,128)(2,1)}), bf16[128,72,128]{2,1,0:T(8,128)(2,1)}, u32[]{:S(2)}, u32[]{:S(2)}) %all-to-all-start.4) | async-done | bytes 2359328 | tf_op jit(solution)/shard_map/all_to_all | solution.py:566
  215.6 4.8 %all-to-all-start.2 = ((bf16[128,96,128]{2,1,0:T(8,128)(2,1)}), bf16[128,96,128]{2,1,0:T(8,128)(2,1)S(1)}, u32[]{:S(2)}, u32[]{:S(2)}) async-start(bf16[128,96,128]{2,1,0:T(8,128)(2,1)} %bitcast.52), calls=%async_computation.2 | async-start | bytes 6291456 | tf_op jit(solution)/shard_map/all_to_all | solution.py:566
  220.5 5.3 %pad_maximum_fusion = bf16[7,720,512]{2,1,0:T(8,128)(2,1)} fusion(bf16[4,720,512]{2,1,0:T(8,128)(2,1)} %get-tuple-element.9, bf16[3,720,512]{2,1,0:T(8,128)(2,1)} %get-tuple-element.8), kind=kLoop, calls=%fused_computation | loop fusion | flops 2580480 | bytes 10321920 | tf_op jit(solution)/shard_map/concatenate | solution.py:624
  225.7 11.3 %reshape.250.refs_3_ = bf16[1,7,720,2,256]{4,3,2,1,0:T(2,128)(2,1)} reshape(bf16[7,720,512]{2,1,0:T(8,128)(2,1)} %pad_maximum_fusion) | data formatting | bytes 10321920 | tf_op jit(solution)/shard_map/reshape | solution.py:626
  237.1 10.5 %inverse.2.refs_2_ = f32[3,1536,512]{2,1,0:T(8,128)} custom-call(bf16[128,3,3,8,128]{4,3,2,1,0:T(8,128)(2,1)} %bitcast.21.refs_0_, bf16[1536,768]{1,0:T(8,128)(2,1)} %bitcast.46), custom_call_target="tpu_custom_call" | custom-call | flops 3623878656 | bytes 4718592 | tf_op jit(solution)/shard_map/inverse/pallas_call | solution.py:40
  247.6 13.1 %all-to-all-done.2 = bf16[128,96,128]{2,1,0:T(8,128)(2,1)S(1)} async-done(((bf16[128,96,128]{2,1,0:T(8,128)(2,1)}), bf16[128,96,128]{2,1,0:T(8,128)(2,1)S(1)}, u32[]{:S(2)}, u32[]{:S(2)}) %all-to-all-start.2) | async-done | bytes 3145760 | tf_op jit(solution)/shard_map/all_to_all | solution.py:566
  262.4 13.9 %inverse.3 = bf16[16,12,96,128]{3,2,1,0:T(8,128)(2,1)} custom-call(bf16[128,4,3,8,128]{4,3,2,1,0:T(8,128)(2,1)} %bitcast.44, bf16[1536,1024]{1,0:T(8,128)(2,1)} %bitcast.43, f32[3,1536,512]{2,1,0:T(8,128)} %inverse.2.refs_2_, bf16[1,7,720,2,256]{4,3,2,1,0:T(2,128)(2,1)} %reshape.250.refs_3_), custom_call_target="tpu_custom_call" | custom-call | flops 4831838208 | bytes 6291456 | tf_op jit(solution)/shard_map/inverse/pallas_call | solution.py:40
  276.3 60.4 %all_to_all.31 = bf16[16,1152,128]{2,1,0:T(8,128)(2,1)S(1)} all-to-all(bf16[16,1152,128]{2,1,0:T(8,128)(2,1)} %bitcast.39), channel_id=1, replica_groups=mesh['lat'=8,'lon'=16] {'lon'}, dimensions={0} | all-to-all | bytes 9437184 | tf_op jit(solution)/shard_map/all_to_all | solution.py:566
  336.8 6.8 %blend.1 = bf16[90,90,256]{2,1,0:T(8,128)(2,1)} custom-call(bf16[4,4,12,96,128]{4,3,2,1,0:T(8,128)(2,1)S(1)} %bitcast.35, bf16[90,90,256]{2,1,0:T(8,128)(2,1)S(1)} %bitcast.37), custom_call_target="tpu_custom_call" | custom-call | flops 132710400 | bytes 13271040 | tf_op jit(solution)/shard_map/blend/pallas_call | solution.py:40
  (52 shorter events, 22.0 us)
Async XLA Ops:
  92.3 38.5 %all-to-all-start.3 = ((bf16[128,72,128]{2,1,0:T(8,128)(2,1)}), bf16[128,72,128]{2,1,0:T(8,128)(2,1)S(1)}, u32[]{:S(2)}, u32[]{:S(2)}) async-start(bf16[128,72,128]{2,1,0:T(8,128)(2,1)} %bitcast.48), calls=%async_computation.3 | async-start | bytes 4718592 | tf_op jit(solution)/shard_map/all_to_all | solution.py:566
  130.9 1.4 copy-start.3
  130.9 7.2 %copy-start.6 = (s32[720]{0:T(1024)S(1)}, s32[720]{0:T(1024)}, u32[]{:S(2)}) copy-start(s32[720]{0:T(1024)} %param.8) | copy-start | bytes 8644
  130.9 7.8 %copy-start.5 = (bf16[2,256,256]{2,1,0:T(8,128)(2,1)S(1)}, bf16[2,256,256]{2,1,0:T(8,128)(2,1)}, u32[]{:S(2)}) copy-start(bf16[2,256,256]{2,1,0:T(8,128)(2,1)} %param.7) | copy-start | bytes 786436
  132.3 45.6 %all-to-all-start.1 = ((bf16[128,96,128]{2,1,0:T(8,128)(2,1)}), bf16[128,96,128]{2,1,0:T(8,128)(2,1)}, u32[]{:S(2)}, u32[]{:S(2)}) async-start(bf16[128,96,128]{2,1,0:T(8,128)(2,1)} %bitcast.40), calls=%async_computation.1 | async-start | bytes 6291456 | tf_op jit(solution)/shard_map/all_to_all | solution.py:566
  138.7 2.6 copy-start.4
  169.5 14.4 %copy-start = (bf16[3,2,128,1536]{3,2,1,0:T(8,128)(2,1)S(1)}, bf16[3,2,128,1536]{3,2,1,0:T(8,128)(2,1)}, u32[]{:S(2)}) copy-start(bf16[3,2,128,1536]{3,2,1,0:T(8,128)(2,1)} %fourier.2.refs_1_) | copy-start | bytes 7077892
  177.9 37.7 %all-to-all-start.4 = ((bf16[128,72,128]{2,1,0:T(8,128)(2,1)}), bf16[128,72,128]{2,1,0:T(8,128)(2,1)}, u32[]{:S(2)}, u32[]{:S(2)}) async-start(bf16[128,72,128]{2,1,0:T(8,128)(2,1)} %bitcast.54), calls=%async_computation.4 | async-start | bytes 4718592 | tf_op jit(solution)/shard_map/all_to_all | solution.py:566
  185.5 4.4 %copy-start.1 = (bf16[4,2,128,1536]{3,2,1,0:T(8,128)(2,1)S(1)}, bf16[4,2,128,1536]{3,2,1,0:T(8,128)(2,1)}, u32[]{:S(2)}) copy-start(bf16[4,2,128,1536]{3,2,1,0:T(8,128)(2,1)} %fourier.3.refs_1_) | copy-start | bytes 9437188
  215.6 45.1 %all-to-all-start.2 = ((bf16[128,96,128]{2,1,0:T(8,128)(2,1)}), bf16[128,96,128]{2,1,0:T(8,128)(2,1)S(1)}, u32[]{:S(2)}, u32[]{:S(2)}) async-start(bf16[128,96,128]{2,1,0:T(8,128)(2,1)} %bitcast.52), calls=%async_computation.2 | async-start | bytes 6291456 | tf_op jit(solution)/shard_map/all_to_all | solution.py:566
  237.1 99.7 %slice-start = ((s8[4423680]{0:T(1024)(128)(4,1)}), s8[229376]{0:T(1024)(128)(4,1)S(1)}, s32[]{:S(2)}) async-start(s8[4423680]{0:T(1024)(128)(4,1)} %bitcast.36), calls=%async_computation.6 | async-start | bytes 458752
  260.7 1.7 copy-start.2
  262.4 74.3 %slice-start.1 = ((s8[4423680]{0:T(1024)(128)(4,1)}), s8[4194304]{0:T(1024)(128)(4,1)S(1)}, s32[]{:S(2)}) async-start(s8[4423680]{0:T(1024)(128)(4,1)} %bitcast.36), calls=%async_computation.7 | async-start | bytes 8388608

commit v3 on v2

--- a/solution.py
+++ b/solution.py
@@ -13,7 +13,6 @@
 UNITS = 3
 PAIRS = UNIT // 2
 LON_PAD = 96
-GROUP = 16
 HALF = 64
 LANES = 128
 SLOTS = 7
@@ -62,12 +61,6 @@
 
 def join_high(first, second):
     return jnp.where(low_half(), swap(first), second)
-
-
-def exchange_rows(outer, inner):
-    row = lax.broadcasted_iota(jnp.int32, (outer * inner, outer * inner), 0)
-    column = lax.broadcasted_iota(jnp.int32, (outer * inner, outer * inner), 1)
-    return (column == (row % inner) * outer + row // inner).astype(jnp.bfloat16)
 
 
 def pack_kernel(band_rows, fields_ref, out_ref):
@@ -115,43 +108,25 @@
     return out.reshape(QUARTERS * QUARTERS, rows // 2, LON_PAD, LANES)
 
 
-def forward_kernel(arrived_ref, table_ref, weight_ref, out_ref, matrix, summed):
+def forward_kernel(arrived_ref, table_ref, weight_ref, out_ref, matrix, turned):
     sources = arrived_ref.shape[0]
     slots, _, owners, longitudes = table_ref.shape
     for pair in range(PAIRS):
         matrix[:, pair * LANES : (pair + 1) * LANES] = arrived_ref[:, pair].reshape(
             sources * LON_PAD, LANES
         )
-    table = table_ref[...].reshape(slots * 2 * owners, longitudes)
-    summed[...] = jnp.dot(table, matrix[...], preferred_element_type=jnp.float32)
-    turn = exchange_rows(GROUP, UNIT)
     weights = weight_ref[0]
 
-    def one_slot(slot, carry):
-        rows = []
-        base = pl.multiple_of(slot * 2 * owners, 2 * owners)
+    for slot in range(slots):
+        table = table_ref[slot].reshape(2 * owners, longitudes)
+        summed = jnp.dot(table, matrix[...], preferred_element_type=jnp.float32)
         for pair in range(PAIRS):
             lanes = slice(pair * LANES, (pair + 1) * LANES)
-            real = summed[pl.ds(base, owners), lanes] * weights[:, lanes]
-            imag = summed[pl.ds(base + owners, owners), lanes] * weights[:, lanes]
-            rows.append(join_low(real, imag).astype(jnp.bfloat16))
-            rows.append(join_high(real, imag).astype(jnp.bfloat16))
-        for first in range(0, owners, 2 * GROUP):
-            both = jnp.concatenate(
-                [
-                    jnp.concatenate([row[start : start + GROUP] for row in rows], axis=0)
-                    for start in (first, first + GROUP)
-                ],
-                axis=1,
-            )
-            both = jnp.dot(turn, both, preferred_element_type=jnp.float32)
-            for half in range(2):
-                piece = both[:, half * LANES : (half + 1) * LANES].reshape(GROUP, UNIT, LANES)
-                start = first + half * GROUP
-                out_ref[start : start + GROUP, slot, 0] = piece.astype(jnp.bfloat16)
-        return carry
-
-    lax.fori_loop(0, slots, one_slot, 0)
+            real = summed[:owners, lanes] * weights[:, lanes]
+            imag = summed[owners:, lanes] * weights[:, lanes]
+            turned[slot, pl.ds(2 * pair, owners, stride=UNIT), :] = join_low(real, imag)
+            turned[slot, pl.ds(2 * pair + 1, owners, stride=UNIT), :] = join_high(real, imag)
+        out_ref[:, slot, 0] = turned[slot].reshape(owners, UNIT, LANES).astype(jnp.bfloat16)
 
 
 def forward(arrived, table, weights, slots, after=()):
@@ -179,7 +154,7 @@
         out_shape=jax.ShapeDtypeStruct((owners, stop - start, UNITS, UNIT, LANES), jnp.bfloat16),
         scratch_shapes=[
             pltpu.VMEM((sources * LON_PAD, PAIRS * LANES), jnp.bfloat16),
-            pltpu.VMEM(((stop - start) * 2 * owners, PAIRS * LANES), jnp.float32),
+            pltpu.VMEM((stop - start, owners * UNIT, LANES), jnp.float32),
         ],
     )
 
@@ -262,44 +237,31 @@
 def inverse_kernel(scale, has_partial, *refs):
     arrived_ref, table_ref = refs[:2]
     partial_ref = refs[2] if has_partial else None
-    out_ref, matrix = refs[-2:]
+    out_ref, matrix, wide = refs[-3:]
     owners, slots = arrived_ref.shape[:2]
 
-    def one_slot(slot, carry):
-        row = pl.multiple_of(slot * 2 * owners, 2 * owners)
-        turn = exchange_rows(UNIT, GROUP)
-        wide = arrived_ref[:, slot, 0].astype(jnp.float32).reshape(owners * UNIT, LANES)
-        wide = wide.astype(jnp.bfloat16)
-        size = GROUP * UNIT
-        groups = []
-        for first in range(0, owners * UNIT, 2 * size):
-            both = jnp.concatenate(
-                [wide[first : first + size], wide[first + size : first + 2 * size]], axis=1
-            )
-            both = jnp.dot(turn, both, preferred_element_type=jnp.float32)
-            groups += [both[:, :LANES], both[:, LANES:]]
+    for slot in range(slots):
+        rows = slice(slot * 2 * owners, (slot * 2 + 1) * owners)
+        more = slice((slot * 2 + 1) * owners, (slot * 2 + 2) * owners)
+        wide[slot] = arrived_ref[:, slot, 0].astype(jnp.float32).reshape(owners * UNIT, LANES)
         for pair in range(PAIRS):
-            one, two = [
-                jnp.concatenate([g[k * GROUP : (k + 1) * GROUP] for g in groups], axis=0)
-                for k in (2 * pair, 2 * pair + 1)
-            ]
+            one = wide[slot, pl.ds(2 * pair, owners, stride=UNIT), :]
+            two = wide[slot, pl.ds(2 * pair + 1, owners, stride=UNIT), :]
             lanes = slice(pair * LANES, (pair + 1) * LANES)
-            matrix[pl.ds(row, owners), lanes] = join_low(one, two).astype(jnp.bfloat16)
-            matrix[pl.ds(row + owners, owners), lanes] = join_high(one, two).astype(
-                jnp.bfloat16
-            )
-        return carry
-
-    lax.fori_loop(0, slots, one_slot, 0)
-
-    summed = jnp.dot(table_ref[...], matrix[...], preferred_element_type=jnp.float32)
-    if not has_partial:
-        out_ref[0] = summed
-        return
-    summed = ((summed + partial_ref[0]) * scale).astype(jnp.bfloat16)
-    for pair in range(PAIRS):
-        lanes = slice(pair * LANES, (pair + 1) * LANES)
-        out_ref[:, pair] = summed[:, lanes].reshape(-1, LON_PAD, LANES)
+            matrix[rows, lanes] = join_low(one, two).astype(jnp.bfloat16)
+            matrix[more, lanes] = join_high(one, two).astype(jnp.bfloat16)
+    blocks = 4
+    for first in range(0, table_ref.shape[0], blocks * LON_PAD):
+        rows = slice(first, first + blocks * LON_PAD)
+        summed = jnp.dot(table_ref[rows], matrix[...], preferred_element_type=jnp.float32)
+        if not has_partial:
+            out_ref[0, rows] = summed
+            continue
+        summed = ((summed + partial_ref[0, rows]) * scale).astype(jnp.bfloat16)
+        place = slice(first // LON_PAD, first // LON_PAD + blocks)
+        for pair in range(PAIRS):
+            lanes = slice(pair * LANES, (pair + 1) * LANES)
+            out_ref[place, pair] = summed[:, lanes].reshape(blocks, LON_PAD, LANES)
 
 
 def inverse(arrived, table, chunk, lon_total, partial=None, after=()):
@@ -331,15 +293,19 @@
         + ([summed] if has_partial else []),
         out_specs=spec,
         out_shape=shape,
-        scratch_shapes=[pltpu.VMEM((table.shape[1], PAIRS * LANES), jnp.bfloat16)],
-    )
+        scratch_shapes=[
+            pltpu.VMEM((table.shape[1], PAIRS * LANES), jnp.bfloat16),
+            pltpu.VMEM((slots, owners * UNIT, LANES), jnp.float32),
+        ],
+    )
+
+
+def gelu(value):
+    return 0.5 * value * (1.0 + lax.erf(value * math.sqrt(0.5)))
 
 
 def blend_kernel(arrived_ref, fields_ref, out_ref):
     lon_cols = fields_ref.shape[1]
-
-    def gelu(value):
-        return 0.5 * value * (1.0 + lax.erf(value * math.sqrt(0.5)))
 
     for pair in range(PAIRS):
         for tile in range(2):
@@ -486,12 +452,12 @@
     slot = first_slot + pl.program_id(0)
     row = lax.broadcasted_iota(jnp.int32, (owners, owners), 0)
     column = lax.broadcasted_iota(jnp.int32, (owners, owners), 1)
-    counts = count_ref[...]
+    counts = count_ref[...].astype(jnp.float32)
     start = jnp.sum(jnp.where(column < row, counts, 0.0), axis=1, keepdims=True)
     count = jnp.sum(jnp.where(column == row, counts, 0.0), axis=1, keepdims=True)
     mode = lax.broadcasted_iota(jnp.int32, (owners, modes), 1).astype(jnp.float32)
     found = mode == start + slot.astype(jnp.float32)
-    order = jnp.sum(jnp.where(found, list_ref[...], 0.0), axis=1, keepdims=True)
+    order = jnp.sum(jnp.where(found, list_ref[...].astype(jnp.float32), 0.0), axis=1, keepdims=True)
     order = jnp.where(slot.astype(jnp.float32) < count, order, -1.0)
     order = jnp.broadcast_to(order, (owners, LANES))
     rest = order - 4.0 * jnp.floor(order * 0.25)
@@ -522,7 +488,7 @@
 def fourier_table(column_list, column_counts, slots, lon_devices, lon_cols, after=()):
     start, stop = slots
     owners = column_counts.shape[0]
-    modes = -(-column_list.shape[0] // LANES) * LANES
+    modes = column_list.shape[0]
     place = jnp.arange(lon_devices * LON_PAD, dtype=jnp.int32)
     block, inside = place // LON_PAD, place % LON_PAD
     longitude = jnp.where(inside < lon_cols, block * lon_cols + inside, -1)
@@ -533,8 +499,8 @@
         20 * math.prod(shape),
         2 * math.prod(shape),
         operands=[
-            jnp.pad(column_list, (0, modes - column_list.shape[0])).astype(jnp.float32)[None, :],
-            column_counts.astype(jnp.float32)[None, :],
+            column_list[None, :],
+            column_counts[None, :],
             longitude.astype(jnp.float32)[None, :],
         ],
         after=after,

time: 345 us -> 338 us (0.980)
  Pallas kernels: 106 us -> 97.2 us
  waiting for transfers between devices: 44.7 us -> 49.4 us
    pallas_call x11, Pallas kernels: 106 us -> 97.2 us  [call(): pl.pallas_call(body, name=name, compiler_params=pltpu.CompilerParams(vmem...]
    all_to_all x4, waiting for transfers between devices: 44.7 us -> 49.4 us  [exchange(): flat = lax.all_to_all(flat, axes, split_axis=0, concat_axis=0, tiled=True)]
  transfers between devices with their start and end apart: 4 -> 4, of which waited for: 4 -> 4; matrix products, arithmetic and copies ran while one was open for 10% -> 11% of each run, Pallas kernels for 19% -> 17%
where the time goes in v3:
time: 338 us; the launch traced here: 337 us
  blocking collectives  125 us (37%)
  Pallas kernels  97.2 us (29%)
  waiting for transfers between devices  49.4 us (15%)
  local copies, waits for them, and re-layouts  30.8 us (9%)
  starting transfers between devices  22.6 us (7%)
  other arithmetic  11.2 us (3%)
    all_to_all x2, blocking collectives, exchange(): flat = lax.all_to_all(flat, axes, split_axis=0, concat_axis=0, tiled=True)  125 us
    pallas_call x11, Pallas kernels, call(): pl.pallas_call(body, name=name, compiler_params=pltpu.CompilerParams(vmem...  97.2 us
    all_to_all x4, waiting for transfers between devices, exchange(): flat = lax.all_to_all(flat, axes, split_axis=0, concat_axis=0, tiled=True)  49.4 us
    all_to_all x4, starting transfers between devices, exchange(): flat = lax.all_to_all(flat, axes, split_axis=0, concat_axis=0, tiled=True)  22.6 us
    reshape x1, local copies, waits for them, and re-layouts, shards(): spectrum = spectrum.reshape(1, SLOTS, degrees, 2, channels)  11.3 us
    reshape x2, local copies, waits for them, and re-layouts, turned(): (table * factor[:, None, :, None]).reshape(-1, lon_devices * LON_PAD)  9.09 us
  transfers between devices with their start and end apart: 4, of which 4 were waited for; matrix products, arithmetic and copies ran while one was open for 11% of the time, Pallas kernels for 17%

profile of v3, /device:TPU:0, one launch (start us, length us, event | category | flops | bytes accessed | tf_op | source)
XLA Modules:
  0.0 337.2 jit_solution(6226789242886380955)
XLA Ops:
  7.1 7.6 %pack.1 = bf16[4,4,12,96,128]{4,3,2,1,0:T(8,128)(2,1)} custom-call(bf16[90,90,256]{2,1,0:T(8,128)(2,1)} %refs_1_.1, bf16[3,2,128,1536]{3,2,1,0:T(8,128)(2,1)} %fourier.2.refs_1_, f32[3,1,512]{2,1,0:T(1,128)} %broadcast_in_dim.63.refs_2_), custom_call_target="tpu_custom_call" | custom-call | bytes 9437184 | tf_op jit(solution)/shard_map/pack/pallas_call | solution.py:39
  14.7 64.7 %all_to_all.30 = bf16[16,1152,128]{2,1,0:T(8,128)(2,1)} all-to-all(bf16[16,1152,128]{2,1,0:T(8,128)(2,1)} %bitcast.37), channel_id=1, replica_groups=mesh['lat'=8,'lon'=16] {'lon'}, dimensions={0} | all-to-all | bytes 9437184 | tf_op jit(solution)/shard_map/all_to_all | solution.py:532
  79.4 8.2 %forward.2.refs_3_ = bf16[128,3,3,8,128]{4,3,2,1,0:T(8,128)(2,1)} custom-call(bf16[16,12,96,128]{3,2,1,0:T(8,128)(2,1)} %bitcast.48, bf16[3,2,128,1536]{3,2,1,0:T(8,128)(2,1)} %fourier.2.refs_1_, f32[3,1,512]{2,1,0:T(1,128)} %broadcast_in_dim.63.refs_2_), custom_call_target="tpu_custom_call" | custom-call | flops 3623878656 | bytes 7077888 | tf_op jit(solution)/shard_map/forward/pallas_call | solution.py:39
  87.7 6.2 %all-to-all-start.3 = ((bf16[128,72,128]{2,1,0:T(8,128)(2,1)}), bf16[128,72,128]{2,1,0:T(8,128)(2,1)S(1)}, u32[]{:S(2)}, u32[]{:S(2)}) async-start(bf16[128,72,128]{2,1,0:T(8,128)(2,1)} %bitcast.47), calls=%async_computation.3 | async-start | bytes 4718592 | tf_op jit(solution)/shard_map/all_to_all | solution.py:532
  93.8 4.5 %fourier.3.refs_1_ = bf16[4,2,128,1536]{3,2,1,0:T(8,128)(2,1)} custom-call(s32[1,720]{1,0:T(1,128)} %broadcast_in_dim.60.refs_0_, s32[1,128]{1,0:T(1,128)} %bitcast.61, f32[1,1536]{1,0:T(1,128)} %fusion.2.refs_2_, bf16[128,3,3,8,128]{4,3,2,1,0:T(8,128)(2,1)} %forward.2.refs_3_), custom_call_target="tpu_custom_call" | custom-call | flops 31457280 | bytes 3145728 | tf_op jit(solution)/shard_map/fourier/pallas_call | solution.py:39
  98.3 9.8 %forward.3.refs_3_ = bf16[128,4,3,8,128]{4,3,2,1,0:T(8,128)(2,1)} custom-call(bf16[16,12,96,128]{3,2,1,0:T(8,128)(2,1)} %bitcast.49, bf16[4,2,128,1536]{3,2,1,0:T(8,128)(2,1)} %fourier.3.refs_1_, f32[3,1,512]{2,1,0:T(1,128)} %broadcast_in_dim.63.refs_2_), custom_call_target="tpu_custom_call" | custom-call | flops 4831838208 | bytes 7864320 | tf_op jit(solution)/shard_map/forward/pallas_call | solution.py:39
  108.2 18.0 %all-to-all-done.3 = bf16[128,72,128]{2,1,0:T(8,128)(2,1)S(1)} async-done(((bf16[128,72,128]{2,1,0:T(8,128)(2,1)}), bf16[128,72,128]{2,1,0:T(8,128)(2,1)S(1)}, u32[]{:S(2)}, u32[]{:S(2)}) %all-to-all-start.3) | async-done | bytes 2359328 | tf_op jit(solution)/shard_map/all_to_all | solution.py:532
  127.6 5.7 %all-to-all-start.1 = ((bf16[128,96,128]{2,1,0:T(8,128)(2,1)}), bf16[128,96,128]{2,1,0:T(8,128)(2,1)}, u32[]{:S(2)}, u32[]{:S(2)}) async-start(bf16[128,96,128]{2,1,0:T(8,128)(2,1)} %bitcast.39), calls=%async_computation.1 | async-start | bytes 6291456 | tf_op jit(solution)/shard_map/all_to_all | solution.py:532
  140.4 16.1 %legendre.1.refs_1_ = bf16[7,768,768]{2,1,0:T(8,128)(2,1)} custom-call(f32[8,128]{1,0:T(8,128)} %broadcast_in_dim.66.refs_0_, f32[8,128]{1,0:T(8,128)} %broadcast_in_dim.67.refs_1_, f32[2,768]{1,0:T(2,128)} %pad_maximum_fusion.1.refs_2_, bf16[128,4,3,8,128]{4,3,2,1,0:T(8,128)(2,1)} %forward.3.refs_3_), custom_call_target="tpu_custom_call" | custom-call | flops 141557760 | bytes 8257536 | tf_op jit(solution)/shard_map/legendre/pallas_call | solution.py:39
  156.5 8.7 %middle.3 = (bf16[3,720,512]{2,1,0:T(8,128)(2,1)}, bf16[32,4,3,3,8,128]{5,4,3,2,1,0:T(8,128)(2,1)}) custom-call(bf16[128,3,3,8,128]{4,3,2,1,0:T(8,128)(2,1)} %bitcast.52, bf16[7,768,768]{2,1,0:T(8,128)(2,1)} %legendre.1.refs_1_, f32[720,512]{1,0:T(8,128)} %bitcast.58, bf16[512,512]{1,0:T(8,128)(2,1)} %copy.33.refs_3_), custom_call_target="tpu_custom_call" | custom-call | flops 4831838208 | bytes 14155776 | tf_op jit(solution)/shard_map/middle/pallas_call | solution.py:39
  165.2 8.0 %all-to-all-done.1 = bf16[128,96,128]{2,1,0:T(8,128)(2,1)} async-done(((bf16[128,96,128]{2,1,0:T(8,128)(2,1)}), bf16[128,96,128]{2,1,0:T(8,128)(2,1)}, u32[]{:S(2)}, u32[]{:S(2)}) %all-to-all-start.1) | async-done | bytes 3145760 | tf_op jit(solution)/shard_map/all_to_all | solution.py:532
  173.2 5.9 %all-to-all-start.4 = ((bf16[128,72,128]{2,1,0:T(8,128)(2,1)}), bf16[128,72,128]{2,1,0:T(8,128)(2,1)}, u32[]{:S(2)}, u32[]{:S(2)}) async-start(bf16[128,72,128]{2,1,0:T(8,128)(2,1)} %bitcast.53), calls=%async_computation.4 | async-start | bytes 4718592 | tf_op jit(solution)/shard_map/all_to_all | solution.py:532
  180.8 4.4 %copy.35 = bf16[768,1536]{0,1:T(8,128)(2,1)} copy(bf16[768,1536]{1,0:T(8,128)(2,1)} %bitcast.46) | data formatting | bytes 4718592 | tf_op jit(solution)/shard_map/reshape | solution.py:572
  187.2 4.7 %copy.36 = bf16[1024,1536]{0,1:T(8,128)(2,1)} copy(bf16[1024,1536]{1,0:T(8,128)(2,1)} %bitcast.40) | data formatting | bytes 6291456 | tf_op jit(solution)/shard_map/reshape | solution.py:572
  191.9 10.6 %middle.2 = (bf16[4,720,512]{2,1,0:T(8,128)(2,1)}, bf16[32,4,4,3,8,128]{5,4,3,2,1,0:T(8,128)(2,1)}) custom-call(bf16[128,4,3,8,128]{4,3,2,1,0:T(8,128)(2,1)} %bitcast.4.refs_0_, bf16[7,768,768]{2,1,0:T(8,128)(2,1)} %legendre.1.refs_1_, f32[720,512]{1,0:T(8,128)} %bitcast.59, bf16[512,512]{1,0:T(8,128)(2,1)} %copy.33.refs_3_, bf16[1536,768]{1,0:T(8,128)(2,1)} %bitcast.44, ...), custom_call_target="tpu_custom_call" | custom-call | flops 6442450944 | bytes 18874368 | tf_op jit(solution)/shard_map/middle/pallas_call | solution.py:39
  202.5 8.7 %all-to-all-done.4 = bf16[128,72,128]{2,1,0:T(8,128)(2,1)} async-done(((bf16[128,72,128]{2,1,0:T(8,128)(2,1)}), bf16[128,72,128]{2,1,0:T(8,128)(2,1)}, u32[]{:S(2)}, u32[]{:S(2)}) %all-to-all-start.4) | async-done | bytes 2359328 | tf_op jit(solution)/shard_map/all_to_all | solution.py:532
  211.1 4.8 %all-to-all-start.2 = ((bf16[128,96,128]{2,1,0:T(8,128)(2,1)}), bf16[128,96,128]{2,1,0:T(8,128)(2,1)S(1)}, u32[]{:S(2)}, u32[]{:S(2)}) async-start(bf16[128,96,128]{2,1,0:T(8,128)(2,1)} %bitcast.51), calls=%async_computation.2 | async-start | bytes 6291456 | tf_op jit(solution)/shard_map/all_to_all | solution.py:532
  216.0 5.3 %pad_maximum_fusion = bf16[7,720,512]{2,1,0:T(8,128)(2,1)} fusion(bf16[4,720,512]{2,1,0:T(8,128)(2,1)} %get-tuple-element.9, bf16[3,720,512]{2,1,0:T(8,128)(2,1)} %get-tuple-element.8), kind=kLoop, calls=%fused_computation | loop fusion | flops 2580480 | bytes 10321920 | tf_op jit(solution)/shard_map/concatenate | solution.py:590
  221.2 11.3 %reshape.250.refs_3_ = bf16[1,7,720,2,256]{4,3,2,1,0:T(2,128)(2,1)} reshape(bf16[7,720,512]{2,1,0:T(8,128)(2,1)} %pad_maximum_fusion) | data formatting | bytes 10321920 | tf_op jit(solution)/shard_map/reshape | solution.py:592
  232.6 8.9 %inverse.2.refs_2_ = f32[3,1536,512]{2,1,0:T(8,128)} custom-call(bf16[128,3,3,8,128]{4,3,2,1,0:T(8,128)(2,1)} %bitcast.21.refs_0_, bf16[1536,768]{1,0:T(8,128)(2,1)} %bitcast.45), custom_call_target="tpu_custom_call" | custom-call | flops 3623878656 | bytes 4718592 | tf_op jit(solution)/shard_map/inverse/pallas_call | solution.py:39
  241.5 14.7 %all-to-all-done.2 = bf16[128,96,128]{2,1,0:T(8,128)(2,1)S(1)} async-done(((bf16[128,96,128]{2,1,0:T(8,128)(2,1)}), bf16[128,96,128]{2,1,0:T(8,128)(2,1)S(1)}, u32[]{:S(2)}, u32[]{:S(2)}) %all-to-all-start.2) | async-done | bytes 3145760 | tf_op jit(solution)/shard_map/all_to_all | solution.py:532
  257.9 12.1 %inverse.3 = bf16[16,12,96,128]{3,2,1,0:T(8,128)(2,1)} custom-call(bf16[128,4,3,8,128]{4,3,2,1,0:T(8,128)(2,1)} %bitcast.43, bf16[1536,1024]{1,0:T(8,128)(2,1)} %bitcast.42, f32[3,1536,512]{2,1,0:T(8,128)} %inverse.2.refs_2_, bf16[1,7,720,2,256]{4,3,2,1,0:T(2,128)(2,1)} %reshape.250.refs_3_), custom_call_target="tpu_custom_call" | custom-call | flops 4831838208 | bytes 6291456 | tf_op jit(solution)/shard_map/inverse/pallas_call | solution.py:39
  270.0 60.4 %all_to_all.31 = bf16[16,1152,128]{2,1,0:T(8,128)(2,1)S(1)} all-to-all(bf16[16,1152,128]{2,1,0:T(8,128)(2,1)} %bitcast.38), channel_id=1, replica_groups=mesh['lat'=8,'lon'=16] {'lon'}, dimensions={0} | all-to-all | bytes 9437184 | tf_op jit(solution)/shard_map/all_to_all | solution.py:532
  330.4 6.8 %blend.1 = bf16[90,90,256]{2,1,0:T(8,128)(2,1)} custom-call(bf16[4,4,12,96,128]{4,3,2,1,0:T(8,128)(2,1)S(1)} %bitcast.34, bf16[90,90,256]{2,1,0:T(8,128)(2,1)S(1)} %bitcast.36), custom_call_target="tpu_custom_call" | custom-call | flops 132710400 | bytes 13271040 | tf_op jit(solution)/shard_map/blend/pallas_call | solution.py:39
  (53 shorter events, 20.1 us)
Async XLA Ops:
  87.7 38.5 %all-to-all-start.3 = ((bf16[128,72,128]{2,1,0:T(8,128)(2,1)}), bf16[128,72,128]{2,1,0:T(8,128)(2,1)S(1)}, u32[]{:S(2)}, u32[]{:S(2)}) async-start(bf16[128,72,128]{2,1,0:T(8,128)(2,1)} %bitcast.47), calls=%async_computation.3 | async-start | bytes 4718592 | tf_op jit(solution)/shard_map/all_to_all | solution.py:532
  126.2 1.4 copy-start.3
  126.2 7.2 %copy-start.7 = (s32[128]{0:T(128)S(1)}, s32[128]{0:T(128)}, u32[]{:S(2)}) copy-start(s32[128]{0:T(128)} %param.9) | copy-start | bytes 1540
  126.2 7.6 %copy-start.6 = (s32[720]{0:T(1024)S(1)}, s32[720]{0:T(1024)}, u32[]{:S(2)}) copy-start(s32[720]{0:T(1024)} %param.8) | copy-start | bytes 8644
  126.2 8.2 %copy-start.5 = (bf16[2,256,256]{2,1,0:T(8,128)(2,1)S(1)}, bf16[2,256,256]{2,1,0:T(8,128)(2,1)}, u32[]{:S(2)}) copy-start(bf16[2,256,256]{2,1,0:T(8,128)(2,1)} %param.7) | copy-start | bytes 786436
  127.6 45.6 %all-to-all-start.1 = ((bf16[128,96,128]{2,1,0:T(8,128)(2,1)}), bf16[128,96,128]{2,1,0:T(8,128)(2,1)}, u32[]{:S(2)}, u32[]{:S(2)}) async-start(bf16[128,96,128]{2,1,0:T(8,128)(2,1)} %bitcast.39), calls=%async_computation.1 | async-start | bytes 6291456 | tf_op jit(solution)/shard_map/all_to_all | solution.py:532
  134.5 2.6 copy-start.4
  165.2 13.9 %copy-start = (bf16[3,2,128,1536]{3,2,1,0:T(8,128)(2,1)S(1)}, bf16[3,2,128,1536]{3,2,1,0:T(8,128)(2,1)}, u32[]{:S(2)}) copy-start(bf16[3,2,128,1536]{3,2,1,0:T(8,128)(2,1)} %fourier.2.refs_1_) | copy-start | bytes 7077892
  173.2 37.9 %all-to-all-start.4 = ((bf16[128,72,128]{2,1,0:T(8,128)(2,1)}), bf16[128,72,128]{2,1,0:T(8,128)(2,1)}, u32[]{:S(2)}, u32[]{:S(2)}) async-start(bf16[128,72,128]{2,1,0:T(8,128)(2,1)} %bitcast.53), calls=%async_computation.4 | async-start | bytes 4718592 | tf_op jit(solution)/shard_map/all_to_all | solution.py:532
  180.8 4.4 %copy-start.1 = (bf16[4,2,128,1536]{3,2,1,0:T(8,128)(2,1)S(1)}, bf16[4,2,128,1536]{3,2,1,0:T(8,128)(2,1)}, u32[]{:S(2)}) copy-start(bf16[4,2,128,1536]{3,2,1,0:T(8,128)(2,1)} %fourier.3.refs_1_) | copy-start | bytes 9437188
  211.1 45.1 %all-to-all-start.2 = ((bf16[128,96,128]{2,1,0:T(8,128)(2,1)}), bf16[128,96,128]{2,1,0:T(8,128)(2,1)S(1)}, u32[]{:S(2)}, u32[]{:S(2)}) async-start(bf16[128,96,128]{2,1,0:T(8,128)(2,1)} %bitcast.51), calls=%async_computation.2 | async-start | bytes 6291456 | tf_op jit(solution)/shard_map/all_to_all | solution.py:532
  232.6 97.8 %slice-start = ((s8[4423680]{0:T(1024)(128)(4,1)}), s8[229376]{0:T(1024)(128)(4,1)S(1)}, s32[]{:S(2)}) async-start(s8[4423680]{0:T(1024)(128)(4,1)} %bitcast.35), calls=%async_computation.6 | async-start | bytes 458752
  256.2 1.7 copy-start.2
  257.9 72.5 %slice-start.1 = ((s8[4423680]{0:T(1024)(128)(4,1)}), s8[4194304]{0:T(1024)(128)(4,1)S(1)}, s32[]{:S(2)}) async-start(s8[4423680]{0:T(1024)(128)(4,1)} %bitcast.35), calls=%async_computation.7 | async-start | bytes 8388608

commit v4 on v3

--- a/solution.py
+++ b/solution.py
@@ -19,7 +19,7 @@
 LEVELS = 768
 ROWS = 768
 HOME_CHUNKS = ((0, 3),)
-SLOT_CHUNKS = ((0, 3), (3, 7))
+SLOT_CHUNKS = ((0, 2), (2, 7))
 VMEM = 60
 SEND_VMEM = 54
 LESS_VMEM = 28
@@ -580,12 +580,12 @@
     send = forward(gathered, late_table, weights, late)
     late_arrived = exchange(send, ("lat", "lon"))
     associated = legendre(own_orders, colatitude, degrees, (send,))
-    early_spectrum, send = middle(early_arrived, associated, gain, mixing, early)
+    early_back, late_back = turned(early_table, early), turned(late_table, late)
+    early_spectrum, send = middle(
+        early_arrived, associated, gain, mixing, early, (early_back, late_back)
+    )
     early_landed = exchange(send, ("lat", "lon"))
-    early_back, late_back = turned(early_table, early), turned(late_table, late)
-    late_spectrum, send = middle(
-        late_arrived, associated, gain, mixing, late, (early_back, late_back)
-    )
+    late_spectrum, send = middle(late_arrived, associated, gain, mixing, late)
     late_landed = exchange(send, ("lat", "lon"))
     spectrum = jnp.concatenate([early_spectrum, late_spectrum])
     partials = [inverse(early_landed, early_back, chunk, lon_total) for chunk in HOME_CHUNKS]

time: 338 us -> 338 us (level)
  transfers between devices with their start and end apart: 4 -> 4, of which waited for: 4 -> 4; matrix products, arithmetic and copies ran while one was open for 11% -> 10% of each run, Pallas kernels for 17% -> 18%
where the time goes in v4:
time: 338 us; the launch traced here: 337 us
  blocking collectives  125 us (37%)
  Pallas kernels  97.3 us (29%)
  waiting for transfers between devices  50.4 us (15%)
  local copies, waits for them, and re-layouts  28.9 us (9%)
  starting transfers between devices  23.4 us (7%)
  other arithmetic  11.1 us (3%)
    all_to_all x2, blocking collectives, exchange(): flat = lax.all_to_all(flat, axes, split_axis=0, concat_axis=0, tiled=True)  125 us
    pallas_call x11, Pallas kernels, call(): pl.pallas_call(body, name=name, compiler_params=pltpu.CompilerParams(vmem...  97.3 us
    all_to_all x4, waiting for transfers between devices, exchange(): flat = lax.all_to_all(flat, axes, split_axis=0, concat_axis=0, tiled=True)  50.4 us
    all_to_all x4, starting transfers between devices, exchange(): flat = lax.all_to_all(flat, axes, split_axis=0, concat_axis=0, tiled=True)  23.4 us
    reshape x1, local copies, waits for them, and re-layouts, shards(): spectrum = spectrum.reshape(1, SLOTS, degrees, 2, channels)  11.4 us
    reshape x2, local copies, waits for them, and re-layouts, turned(): (table * factor[:, None, :, None]).reshape(-1, lon_devices * LON_PAD)  7.94 us
  transfers between devices with their start and end apart: 4, of which 4 were waited for; matrix products, arithmetic and copies ran while one was open for 10% of the time, Pallas kernels for 18%

profile of v4, /device:TPU:0, one launch (start us, length us, event | category | flops | bytes accessed | tf_op | source)
XLA Modules:
  0.0 337.1 jit_solution(1826345192660133980)
XLA Ops:
  6.3 7.6 %pack.1 = bf16[4,4,12,96,128]{4,3,2,1,0:T(8,128)(2,1)} custom-call(bf16[90,90,256]{2,1,0:T(8,128)(2,1)} %refs_1_.1, bf16[2,2,128,1536]{3,2,1,0:T(8,128)(2,1)} %fourier.2.refs_1_, f32[3,1,512]{2,1,0:T(1,128)} %broadcast_in_dim.63.refs_2_), custom_call_target="tpu_custom_call" | custom-call | bytes 9437184 | tf_op jit(solution)/shard_map/pack/pallas_call | solution.py:39
  13.9 64.7 %all_to_all.30 = bf16[16,1152,128]{2,1,0:T(8,128)(2,1)} all-to-all(bf16[16,1152,128]{2,1,0:T(8,128)(2,1)} %bitcast.39), channel_id=1, replica_groups=mesh['lat'=8,'lon'=16] {'lon'}, dimensions={0} | all-to-all | bytes 9437184 | tf_op jit(solution)/shard_map/all_to_all | solution.py:532
  78.6 6.9 %forward.2.refs_3_ = bf16[128,2,3,8,128]{4,3,2,1,0:T(8,128)(2,1)} custom-call(bf16[16,12,96,128]{3,2,1,0:T(8,128)(2,1)} %bitcast.51, bf16[2,2,128,1536]{3,2,1,0:T(8,128)(2,1)} %fourier.2.refs_1_, f32[3,1,512]{2,1,0:T(1,128)} %broadcast_in_dim.63.refs_2_), custom_call_target="tpu_custom_call" | custom-call | flops 2415919104 | bytes 6291456 | tf_op jit(solution)/shard_map/forward/pallas_call | solution.py:39
  85.5 6.2 %all-to-all-start.3 = ((bf16[128,48,128]{2,1,0:T(8,128)(2,1)}), bf16[128,48,128]{2,1,0:T(8,128)(2,1)S(1)}, u32[]{:S(2)}, u32[]{:S(2)}) async-start(bf16[128,48,128]{2,1,0:T(8,128)(2,1)} %bitcast.47), calls=%async_computation.3 | async-start | bytes 3145728 | tf_op jit(solution)/shard_map/all_to_all | solution.py:532
  91.6 5.4 %fourier.3.refs_1_ = bf16[5,2,128,1536]{3,2,1,0:T(8,128)(2,1)} custom-call(s32[1,720]{1,0:T(1,128)} %broadcast_in_dim.60.refs_0_, s32[1,128]{1,0:T(1,128)} %bitcast.61, f32[1,1536]{1,0:T(1,128)} %fusion.2.refs_2_, bf16[128,2,3,8,128]{4,3,2,1,0:T(8,128)(2,1)} %forward.2.refs_3_), custom_call_target="tpu_custom_call" | custom-call | flops 39321600 | bytes 3932160 | tf_op jit(solution)/shard_map/fourier/pallas_call | solution.py:39
  97.0 11.4 %forward.3.refs_3_ = bf16[128,5,3,8,128]{4,3,2,1,0:T(8,128)(2,1)} custom-call(bf16[16,12,96,128]{3,2,1,0:T(8,128)(2,1)} %bitcast.52, bf16[5,2,128,1536]{3,2,1,0:T(8,128)(2,1)} %fourier.3.refs_1_, f32[3,1,512]{2,1,0:T(1,128)} %broadcast_in_dim.63.refs_2_), custom_call_target="tpu_custom_call" | custom-call | flops 6039797760 | bytes 8650752 | tf_op jit(solution)/shard_map/forward/pallas_call | solution.py:39
  108.4 7.6 %all-to-all-done.3 = bf16[128,48,128]{2,1,0:T(8,128)(2,1)S(1)} async-done(((bf16[128,48,128]{2,1,0:T(8,128)(2,1)}), bf16[128,48,128]{2,1,0:T(8,128)(2,1)S(1)}, u32[]{:S(2)}, u32[]{:S(2)}) %all-to-all-start.3) | async-done | bytes 1572896 | tf_op jit(solution)/shard_map/all_to_all | solution.py:532
  117.2 5.9 %all-to-all-start.1 = ((bf16[128,120,128]{2,1,0:T(8,128)(2,1)}), bf16[128,120,128]{2,1,0:T(8,128)(2,1)}, u32[]{:S(2)}, u32[]{:S(2)}) async-start(bf16[128,120,128]{2,1,0:T(8,128)(2,1)} %bitcast.42), calls=%async_computation.1 | async-start | bytes 7864320 | tf_op jit(solution)/shard_map/all_to_all | solution.py:532
  130.7 4.4 %broadcast_multiply_fusion = bf16[5,2,128,1536]{3,2,1,0:T(8,128)(2,1)} fusion(bf16[5,2,128,1536]{3,2,1,0:T(8,128)(2,1)} %fourier.3.refs_1_, bf16[5,128]{1,0:T(8,128)(2,1)S(1)} %select_convert_fusion), kind=kLoop, calls=%fused_computation.3 | loop fusion | flops 1966080 | bytes 7865600 | tf_op jit(solution)/shard_map/mul | solution.py:572
  135.1 6.3 %copy.35 = bf16[1280,1536]{0,1:T(8,128)(2,1)} copy(bf16[1280,1536]{1,0:T(8,128)(2,1)} %bitcast.41) | data formatting | bytes 7864320 | tf_op jit(solution)/shard_map/reshape | solution.py:572
  142.7 16.2 %legendre.1.refs_1_ = bf16[7,768,768]{2,1,0:T(8,128)(2,1)} custom-call(f32[8,128]{1,0:T(8,128)} %broadcast_in_dim.66.refs_0_, f32[8,128]{1,0:T(8,128)} %broadcast_in_dim.67.refs_1_, f32[2,768]{1,0:T(2,128)} %pad_maximum_fusion.1.refs_2_, bf16[128,5,3,8,128]{4,3,2,1,0:T(8,128)(2,1)} %forward.3.refs_3_), custom_call_target="tpu_custom_call" | custom-call | flops 141557760 | bytes 8257536 | tf_op jit(solution)/shard_map/legendre/pallas_call | solution.py:39
  158.9 6.8 %middle.3 = (bf16[2,720,512]{2,1,0:T(8,128)(2,1)}, bf16[32,4,2,3,8,128]{5,4,3,2,1,0:T(8,128)(2,1)}) custom-call(bf16[128,2,3,8,128]{4,3,2,1,0:T(8,128)(2,1)} %bitcast.45, bf16[7,768,768]{2,1,0:T(8,128)(2,1)} %legendre.1.refs_1_, f32[720,512]{1,0:T(8,128)} %bitcast.49, bf16[512,512]{1,0:T(8,128)(2,1)} %copy.31.refs_3_, bf16[1536,512]{1,0:T(8,128)(2,1)} %bitcast.43, ...), custom_call_target="tpu_custom_call" | custom-call | flops 3221225472 | bytes 9437184 | tf_op jit(solution)/shard_map/middle/pallas_call | solution.py:39
  165.7 5.7 %all-to-all-done.1 = bf16[128,120,128]{2,1,0:T(8,128)(2,1)} async-done(((bf16[128,120,128]{2,1,0:T(8,128)(2,1)}), bf16[128,120,128]{2,1,0:T(8,128)(2,1)}, u32[]{:S(2)}, u32[]{:S(2)}) %all-to-all-start.1) | async-done | bytes 3932192 | tf_op jit(solution)/shard_map/all_to_all | solution.py:532
  171.5 5.3 %all-to-all-start.4 = ((bf16[128,48,128]{2,1,0:T(8,128)(2,1)}), bf16[128,48,128]{2,1,0:T(8,128)(2,1)S(1)}, u32[]{:S(2)}, u32[]{:S(2)}) async-start(bf16[128,48,128]{2,1,0:T(8,128)(2,1)} %bitcast.58), calls=%async_computation.4 | async-start | bytes 3145728 | tf_op jit(solution)/shard_map/all_to_all | solution.py:532
  176.8 12.5 %middle.2 = (bf16[5,720,512]{2,1,0:T(8,128)(2,1)}, bf16[32,4,5,3,8,128]{5,4,3,2,1,0:T(8,128)(2,1)}) custom-call(bf16[128,5,3,8,128]{4,3,2,1,0:T(8,128)(2,1)} %bitcast.4.refs_0_, bf16[7,768,768]{2,1,0:T(8,128)(2,1)} %legendre.1.refs_1_, f32[720,512]{1,0:T(8,128)} %bitcast.50, bf16[512,512]{1,0:T(8,128)(2,1)} %copy.31.refs_3_), custom_call_target="tpu_custom_call" | custom-call | flops 8053063680 | bytes 23592960 | tf_op jit(solution)/shard_map/middle/pallas_call | solution.py:39
  189.3 11.9 %all-to-all-done.4 = bf16[128,48,128]{2,1,0:T(8,128)(2,1)S(1)} async-done(((bf16[128,48,128]{2,1,0:T(8,128)(2,1)}), bf16[128,48,128]{2,1,0:T(8,128)(2,1)S(1)}, u32[]{:S(2)}, u32[]{:S(2)}) %all-to-all-start.4) | async-done | bytes 1572896 | tf_op jit(solution)/shard_map/all_to_all | solution.py:532
  202.4 6.0 %all-to-all-start.2 = ((bf16[128,120,128]{2,1,0:T(8,128)(2,1)}), bf16[128,120,128]{2,1,0:T(8,128)(2,1)}, u32[]{:S(2)}, u32[]{:S(2)}) async-start(bf16[128,120,128]{2,1,0:T(8,128)(2,1)} %bitcast.54), calls=%async_computation.2 | async-start | bytes 7864320 | tf_op jit(solution)/shard_map/all_to_all | solution.py:532
  208.3 7.6 %inverse.2.refs_2_ = f32[3,1536,512]{2,1,0:T(8,128)} custom-call(bf16[128,2,3,8,128]{4,3,2,1,0:T(8,128)(2,1)} %bitcast.46, bf16[1536,512]{1,0:T(8,128)(2,1)} %bitcast.44), custom_call_target="tpu_custom_call" | custom-call | flops 2415919104 | bytes 3145728 | tf_op jit(solution)/shard_map/inverse/pallas_call | solution.py:39
  215.9 4.2 %pad_maximum_fusion = bf16[7,720,512]{2,1,0:T(8,128)(2,1)} fusion(bf16[5,720,512]{2,1,0:T(8,128)(2,1)S(1)} %copy-done.3, bf16[2,720,512]{2,1,0:T(8,128)(2,1)} %get-tuple-element.8), kind=kLoop, calls=%fused_computation | loop fusion | flops 2580480 | bytes 10321920 | tf_op jit(solution)/shard_map/concatenate | solution.py:590
  220.1 11.4 %reshape.250.refs_3_ = bf16[1,7,720,2,256]{4,3,2,1,0:T(2,128)(2,1)} reshape(bf16[7,720,512]{2,1,0:T(8,128)(2,1)} %pad_maximum_fusion) | data formatting | bytes 10321920 | tf_op jit(solution)/shard_map/reshape | solution.py:592
  231.5 25.1 %all-to-all-done.2 = bf16[128,120,128]{2,1,0:T(8,128)(2,1)} async-done(((bf16[128,120,128]{2,1,0:T(8,128)(2,1)}), bf16[128,120,128]{2,1,0:T(8,128)(2,1)}, u32[]{:S(2)}, u32[]{:S(2)}) %all-to-all-start.2) | async-done | bytes 3932192 | tf_op jit(solution)/shard_map/all_to_all | solution.py:532
  256.6 13.2 %inverse.3 = bf16[16,12,96,128]{3,2,1,0:T(8,128)(2,1)} custom-call(bf16[128,5,3,8,128]{4,3,2,1,0:T(8,128)(2,1)} %bitcast.13.refs_0_, bf16[1536,1280]{1,0:T(8,128)(2,1)} %bitcast.38, f32[3,1536,512]{2,1,0:T(8,128)} %inverse.2.refs_2_, bf16[1,7,720,2,256]{4,3,2,1,0:T(2,128)(2,1)} %reshape.250.refs_3_), custom_call_target="tpu_custom_call" | custom-call | flops 6039797760 | bytes 7864320 | tf_op jit(solution)/shard_map/inverse/pallas_call | solution.py:39
  269.8 60.5 %all_to_all.31 = bf16[16,1152,128]{2,1,0:T(8,128)(2,1)S(1)} all-to-all(bf16[16,1152,128]{2,1,0:T(8,128)(2,1)} %bitcast.40), channel_id=1, replica_groups=mesh['lat'=8,'lon'=16] {'lon'}, dimensions={0} | all-to-all | bytes 9437184 | tf_op jit(solution)/shard_map/all_to_all | solution.py:532
  330.3 6.8 %blend.1 = bf16[90,90,256]{2,1,0:T(8,128)(2,1)} custom-call(bf16[4,4,12,96,128]{4,3,2,1,0:T(8,128)(2,1)S(1)} %bitcast.34, bf16[90,90,256]{2,1,0:T(8,128)(2,1)S(1)} %bitcast.36), custom_call_target="tpu_custom_call" | custom-call | flops 132710400 | bytes 13271040 | tf_op jit(solution)/shard_map/blend/pallas_call | solution.py:39
  (53 shorter events, 16.7 us)
Async XLA Ops:
  85.5 30.6 %all-to-all-start.3 = ((bf16[128,48,128]{2,1,0:T(8,128)(2,1)}), bf16[128,48,128]{2,1,0:T(8,128)(2,1)S(1)}, u32[]{:S(2)}, u32[]{:S(2)}) async-start(bf16[128,48,128]{2,1,0:T(8,128)(2,1)} %bitcast.47), calls=%async_computation.3 | async-start | bytes 3145728 | tf_op jit(solution)/shard_map/all_to_all | solution.py:532
  116.1 1.1 copy-start.1
  116.1 7.1 %copy-start.7 = (s32[128]{0:T(128)S(1)}, s32[128]{0:T(128)}, u32[]{:S(2)}) copy-start(s32[128]{0:T(128)} %param.9) | copy-start | bytes 1540
  116.1 7.5 %copy-start.6 = (s32[720]{0:T(1024)S(1)}, s32[720]{0:T(1024)}, u32[]{:S(2)}) copy-start(s32[720]{0:T(1024)} %param.8) | copy-start | bytes 8644
  116.1 8.2 %copy-start.4 = (f32[720,2,256]{2,1,0:T(2,128)S(1)}, f32[720,2,256]{2,1,0:T(2,128)}, u32[]{:S(2)}) copy-start(f32[720,2,256]{2,1,0:T(2,128)} %param.6) | copy-start | bytes 4423684
  116.1 9.5 %copy-start.5 = (bf16[2,256,256]{2,1,0:T(8,128)(2,1)S(1)}, bf16[2,256,256]{2,1,0:T(8,128)(2,1)}, u32[]{:S(2)}) copy-start(bf16[2,256,256]{2,1,0:T(8,128)(2,1)} %param.7) | copy-start | bytes 786436
  117.2 54.2 %all-to-all-start.1 = ((bf16[128,120,128]{2,1,0:T(8,128)(2,1)}), bf16[128,120,128]{2,1,0:T(8,128)(2,1)}, u32[]{:S(2)}, u32[]{:S(2)}) async-start(bf16[128,120,128]{2,1,0:T(8,128)(2,1)} %bitcast.42), calls=%async_computation.1 | async-start | bytes 7864320 | tf_op jit(solution)/shard_map/all_to_all | solution.py:532
  125.6 2.6 copy-start
  171.5 29.7 %all-to-all-start.4 = ((bf16[128,48,128]{2,1,0:T(8,128)(2,1)}), bf16[128,48,128]{2,1,0:T(8,128)(2,1)S(1)}, u32[]{:S(2)}, u32[]{:S(2)}) async-start(bf16[128,48,128]{2,1,0:T(8,128)(2,1)} %bitcast.58), calls=%async_computation.4 | async-start | bytes 3145728 | tf_op jit(solution)/shard_map/all_to_all | solution.py:532
  201.2 1.2 copy-start.2
  202.4 54.2 %all-to-all-start.2 = ((bf16[128,120,128]{2,1,0:T(8,128)(2,1)}), bf16[128,120,128]{2,1,0:T(8,128)(2,1)}, u32[]{:S(2)}, u32[]{:S(2)}) async-start(bf16[128,120,128]{2,1,0:T(8,128)(2,1)} %bitcast.54), calls=%async_computation.2 | async-start | bytes 7864320 | tf_op jit(solution)/shard_map/all_to_all | solution.py:532
  208.3 7.6 %copy-start.3 = (bf16[5,720,512]{2,1,0:T(8,128)(2,1)S(1)}, bf16[5,720,512]{2,1,0:T(8,128)(2,1)}, u32[]{:S(2)}) copy-start(bf16[5,720,512]{2,1,0:T(8,128)(2,1)} %get-tuple-element.9) | copy-start | bytes 11059204
  220.1 110.2 %slice-start = ((s8[4423680]{0:T(1024)(128)(4,1)}), s8[229376]{0:T(1024)(128)(4,1)S(1)}, s32[]{:S(2)}) async-start(s8[4423680]{0:T(1024)(128)(4,1)} %bitcast.35), calls=%async_computation.6 | async-start | bytes 458752
  256.6 73.7 %slice-start.1 = ((s8[4423680]{0:T(1024)(128)(4,1)}), s8[4194304]{0:T(1024)(128)(4,1)S(1)}, s32[]{:S(2)}) async-start(s8[4423680]{0:T(1024)(128)(4,1)} %bitcast.35), calls=%async_computation.7 | async-start | bytes 8388608
